TPU v7x, 32 devices: a whole 2x2x4 slice. The times are simulated.
32 devices in a mesh: pipe: 2 (over core), expert: 16 (over z, y, x).
Axes of the slice: x: 2, y: 2, z: 4, core: 2. Of those that a mesh axis runs over, the one named last changes fastest.
Arguments:
- grad_out: bfloat16 [2, 2, 1024, 2048], P('pipe', None, 'expert'), may hold values from -6 to 6
- route_weights: float32 [2, 2, 1024, 8], P('pipe', None, 'expert'), may hold values from 0.1 to 0.6
- expert_ids: int32 [2, 2, 1024, 8], P('pipe', None, 'expert'), may hold values from 0 to 15, all different within a row; in each aligned block of 64 rows (0 to 63, 64 to 127, ..., all dimensions but the last counted through in order) at most 40 rows name the same one
- hot_pos: int32 [2, 4], P('pipe'), may hold values from 0 to 3, as said below
- up_weight: bfloat16 [2, 16, 2048, 768], P('pipe', 'expert'), may hold values from -0.125 to 0.125
- down_weight: bfloat16 [2, 16, 768, 2048], P('pipe', 'expert'), may hold values from -0.21875 to 0.21875
- saved_inputs: bfloat16 [2, 2, 16, 16, 50, 2048], P('pipe', None, 'expert'), may hold values from -6 to 6
- saved_gates: bfloat16 [2, 2, 16, 16, 50, 768], P('pipe', None, 'expert'), may hold values from -8 to 8
Outputs:
- sent_back: bfloat16 [2, 2, 1024, 2048], P('pipe', None, 'expert')
- up_grad: bfloat16 [2, 16, 2048, 768], P('pipe', 'expert')
- down_grad: bfloat16 [2, 16, 768, 2048], P('pipe', 'expert')
- gate_grads: bfloat16 [2, 2, 16, 16, 50, 768], P('pipe', None, 'expert')
- hot_up_grad: bfloat16 [2, 16, 512, 768], P('pipe', 'expert')
- hot_down_grad: bfloat16 [2, 16, 192, 2048], P('pipe', 'expert')
Inputs may be any that keep to these rules, and one draw needn't show every extreme that they name: `expert_ids`: each token names 8 different experts. Among the rows of one device in one micro-batch of one section no expert is named more than 40 times, a bound that some block reaches. `hot_pos`: in section 0 the first and the last group copy their expert 4 - 2; in section 1 the first group copies its expert 4 - 1 and the last group its expert 4 - 3.
All inputs are finite; a program needn't handle non-finite values.
Results may differ from a plain program's by a relative error of at most 0.0065.
Values may be sent and summed in bfloat16 or wider, within the bound.
A program may use at most 192 MiB of HBM per device.

v0:
```python
import jax
import jax.numpy as jnp
from jax import lax
from jax.sharding import PartitionSpec as P

TOP = 8
REPL = 4
MB = 2


def partner(value, axis, bit):
    mask = 2**bit
    pairs = [(source, source ^ mask) for source in range(lax.axis_size(axis))]
    return lax.ppermute(value, axis, pairs)


def from_behind(block, axis, distance):
    devices = range(lax.axis_size(axis))
    route = [((i - distance) % len(devices), i) for i in devices]
    return lax.ppermute(block, axis, route)


def route_slots(expert_row, sender, hot_table, num_experts, most_rows, slot_count):
    onehot = (expert_row[:, None] == jnp.arange(num_experts, dtype=jnp.int32)[None, :]).astype(
        jnp.int32
    )
    order_pos = jnp.sum(jnp.cumsum(onehot, axis=0) * onehot, axis=1) - 1
    group_id = expert_row // REPL
    hot_count = hot_table.shape[0]
    owner_pos = jnp.sum(
        (group_id[:, None] == jnp.arange(hot_count, dtype=jnp.int32)[None, :]).astype(jnp.int32)
        * hot_table[None, :],
        axis=1,
    )
    is_hot = expert_row % REPL == owner_pos
    target = jnp.where(is_hot, REPL * group_id + (sender + order_pos) % REPL, expert_row)
    slot_pos = jnp.where(is_hot, most_rows + order_pos // REPL, order_pos)
    return target * slot_count + slot_pos


def expert_rows(grad_rows, input_rows, gate_rows, up_w, down_w):
    up_value = jnp.dot(input_rows, up_w, preferred_element_type=jnp.float32)
    gate_value = gate_rows.astype(jnp.float32)
    gate_sig = jax.nn.sigmoid(gate_value)
    active = gate_value * gate_sig
    hidden = (active * up_value).astype(jnp.bfloat16)
    grad_hidden = lax.dot_general(
        grad_rows, down_w, (((1,), (1,)), ((), ())), preferred_element_type=jnp.float32
    )
    grad_up = (grad_hidden * active).astype(jnp.bfloat16)
    grad_gate = (grad_hidden * up_value * gate_sig * (1.0 + gate_value * (1.0 - gate_sig))).astype(
        jnp.bfloat16
    )
    back_rows = lax.dot_general(
        grad_up, up_w, (((1,), (1,)), ((), ())), preferred_element_type=jnp.float32
    ).astype(jnp.bfloat16)
    down_term = lax.dot_general(
        hidden, grad_rows, (((0,), (0,)), ((), ())), preferred_element_type=jnp.float32
    )
    up_term = lax.dot_general(
        input_rows, grad_up, (((0,), (0,)), ((), ())), preferred_element_type=jnp.float32
    )
    return (back_rows, grad_gate, up_term, down_term)


def take_part(matrix, index, parts):
    length = matrix.shape[0] // parts
    return lax.dynamic_slice_in_dim(matrix, index * length, length, 0)


def per_device(
    grad_out, route_weights, expert_ids, hot_pos, up_weight, down_weight, saved_inputs, saved_gates
):
    experts = lax.axis_size("expert")
    device = lax.axis_index("expert")
    features = grad_out.shape[-1]
    hidden_units = saved_gates.shape[-1]
    token_count = grad_out.shape[2]
    slot_count = saved_inputs.shape[4]
    quarter_rows = slot_count // (REPL + 1)
    most_rows = REPL * quarter_rows
    hot_table = hot_pos[0]
    group_id = device // REPL
    local_pos = device % REPL
    low_bit = local_pos % 2
    high_bit = local_pos // 2
    owner_pos = jnp.sum(
        jnp.where(jnp.arange(hot_table.shape[0], dtype=jnp.int32) == group_id, hot_table, 0)
    )
    is_owner = local_pos == owner_pos
    own_up = up_weight[0, 0]
    own_down = down_weight[0, 0]
    owner_mask = is_owner.astype(jnp.bfloat16)
    masked = (own_up * owner_mask, own_down * owner_mask)
    from_low = partner((masked[0], masked[1]), "expert", 0)
    step_one = (masked[0] + from_low[0], masked[1] + from_low[1])
    second = partner((step_one[0], step_one[1]), "expert", 1)
    hot_up = step_one[0] + second[0]
    hot_down = step_one[1] + second[1]
    outputs = []
    token_grads = []
    for batch_idx in range(MB):
        expert_row = expert_ids[0, batch_idx].reshape(-1)
        token_flat_index = route_slots(
            expert_row, device, hot_table, experts, most_rows, slot_count
        )
        scaled = (
            route_weights[0, batch_idx][:, :, None]
            * grad_out[0, batch_idx][:, None, :].astype(jnp.float32)
        ).astype(jnp.bfloat16)
        routed_rows = scaled.reshape(-1, features)
        buffer = (
            jnp.zeros((experts * slot_count, features), jnp.bfloat16)
            .at[token_flat_index]
            .set(routed_rows)
        )
        flat_index, buffer = (token_flat_index, buffer.reshape(experts, slot_count, features))
        received = lax.all_to_all(buffer, "expert", split_axis=0, concat_axis=0, tiled=True)
        inputs_batch = saved_inputs[0, batch_idx, 0]
        gates_batch = saved_gates[0, batch_idx, 0]
        first_part = expert_rows(
            received[:, :most_rows].reshape(-1, features),
            inputs_batch[:, :most_rows].reshape(-1, features),
            gates_batch[:, :most_rows].reshape(-1, hidden_units),
            own_up,
            own_down,
        )
        expert_second = expert_rows(
            received[:, most_rows:].reshape(-1, features),
            inputs_batch[:, most_rows:].reshape(-1, features),
            gates_batch[:, most_rows:].reshape(-1, hidden_units),
            hot_up,
            hot_down,
        )
        back = jnp.concatenate(
            [
                first_part[0].reshape(experts, most_rows, features),
                expert_second[0].reshape(experts, quarter_rows, features),
            ],
            1,
        )
        gate_grad = jnp.concatenate(
            [
                first_part[1].reshape(experts, most_rows, hidden_units),
                expert_second[1].reshape(experts, quarter_rows, hidden_units),
            ],
            1,
        )
        results = (
            back,
            gate_grad,
            first_part[2],
            first_part[3],
            expert_second[2],
            expert_second[3],
        )
        outputs.append(results)
        returned = lax.all_to_all(results[0], "expert", split_axis=0, concat_axis=0, tiled=True)
        gathered = returned.reshape(experts * slot_count, features)[flat_index]
        summed = jnp.sum(gathered.reshape(token_count, TOP, features).astype(jnp.float32), axis=1)
        token_grads.append(
            (summed + grad_out[0, batch_idx].astype(jnp.float32)).astype(jnp.bfloat16)
        )
    own_up_sum = jnp.zeros((features, hidden_units), jnp.float32)
    own_down_sum = jnp.zeros((hidden_units, features), jnp.float32)
    rep_up_sum = jnp.zeros((features, hidden_units), jnp.float32)
    rep_down_sum = jnp.zeros((hidden_units, features), jnp.float32)
    for member in outputs:
        own_up_sum = own_up_sum + member[2]
        own_down_sum = own_down_sum + member[3]
        rep_up_sum = rep_up_sum + member[4]
        rep_down_sum = rep_down_sum + member[5]
    sent_back = from_behind(jnp.stack(token_grads, 0), "pipe", -1)
    rep_terms = (rep_up_sum.astype(jnp.bfloat16), rep_down_sum.astype(jnp.bfloat16))
    outgoing = (take_part(rep_terms[0], 1 - high_bit, 2), take_part(rep_terms[1], 1 - high_bit, 2))
    incoming = partner((outgoing[0], outgoing[1]), "expert", 1)
    halves = (
        take_part(rep_terms[0], high_bit, 2).astype(jnp.float32) + incoming[0].astype(jnp.float32),
        take_part(rep_terms[1], high_bit, 2).astype(jnp.float32) + incoming[1].astype(jnp.float32),
    )
    outgoing = (take_part(halves[0], 1 - low_bit, 2), take_part(halves[1], 1 - low_bit, 2))
    incoming = partner((outgoing[0], outgoing[1]), "expert", 0)
    hot_up_part = (take_part(halves[0], low_bit, 2) + incoming[0]).astype(jnp.bfloat16)
    hot_down_part = (take_part(halves[1], low_bit, 2) + incoming[1]).astype(jnp.bfloat16)
    up_grad = own_up_sum.astype(jnp.bfloat16)
    down_grad = own_down_sum.astype(jnp.bfloat16)
    gate_grads = jnp.stack([member[1] for member in outputs], 0)
    return (
        sent_back[None],
        up_grad[None, None],
        down_grad[None, None],
        gate_grads[None, :, None],
        hot_up_part[None, None],
        hot_down_part[None, None],
    )


def solution(mesh):
    return jax.shard_map(
        per_device,
        mesh=mesh,
        in_specs=(
            P("pipe", None, "expert", None),
            P("pipe", None, "expert", None),
            P("pipe", None, "expert", None),
            P("pipe", None),
            P("pipe", "expert", None, None),
            P("pipe", "expert", None, None),
            P("pipe", None, "expert", None, None, None),
            P("pipe", None, "expert", None, None, None),
        ),
        out_specs=(
            P("pipe", None, "expert", None),
            P("pipe", "expert", None, None),
            P("pipe", "expert", None, None),
            P("pipe", None, "expert", None, None, None),
            P("pipe", "expert", None, None),
            P("pipe", "expert", None, None),
        ),
        check_vma=False,
    )
```

profile of v0, /device:TPU:0, one launch (start us, length us, event | category | flops | bytes accessed | tf_op | source)
XLA Modules:
  0.0 571.5 jit_solution(6725910092687759949)
XLA Ops:
  9.0 5.2 scatter_custom_fusion
  16.9 8.6 %all-to-all-start = ((bf16[16,50,2048]{2,1,0:T(8,128)(2,1)}), bf16[16,50,2048]{2,1,0:T(8,128)(2,1)}, u32[]{:S(2)}, u32[]{:S(2)}) async-start(bf16[16,50,2048]{2,1,0:T(8,128)(2,1)} %reshape.671), calls=%async_computation | async-start | bytes 7340032 | tf_op jit(solution)/shard_map/all_to_all | solution.py:118
  33.8 5.4 scatter_custom_fusion.1
  41.9 5.5 fusion.73
  47.4 48.3 %all-to-all-done = bf16[16,50,2048]{2,1,0:T(8,128)(2,1)} async-done(((bf16[16,50,2048]{2,1,0:T(8,128)(2,1)}), bf16[16,50,2048]{2,1,0:T(8,128)(2,1)}, u32[]{:S(2)}, u32[]{:S(2)}) %all-to-all-start) | async-done | bytes 3276832 | tf_op jit(solution)/shard_map/all_to_all | solution.py:118
  95.7 17.8 %all-to-all-start.2 = ((bf16[16,50,2048]{2,1,0:T(8,128)(2,1)}), bf16[16,50,2048]{2,1,0:T(8,128)(2,1)}, u32[]{:S(2)}, u32[]{:S(2)}) async-start(bf16[16,50,2048]{2,1,0:T(8,128)(2,1)} %reshape.678), calls=%async_computation.2 | async-start | bytes 7340032 | tf_op jit(solution)/shard_map/all_to_all | solution.py:118
  113.6 7.5 %copy_bitcast_fusion = (bf16[16,50,2048]{2,1,0:T(8,128)(2,1)}, bf16[16,50,2048]{2,1,0:T(8,128)(2,1)S(1)}) fusion(bf16[1,1,1,16,50,2048]{5,3,4,2,1,0:T(8,128)(2,1)S(1)} %get-tuple-element.26, bf16[1,1,1,16,50,2048]{5,3,4,2,1,0:T(8,128)(2,1)} %get-tuple-element.27), kind=kLoop, calls=%fused_computation.16 | loop fusion | bytes 13107200 | tf_op jit(solution)/shard_map/squeeze | solution.py:119
  123.8 12.3 %collective-permute-done.2 = bf16[2048,768]{1,0:T(8,128)(2,1)} collective-permute-done((bf16[2048,768]{1,0:T(8,128)(2,1)}, bf16[2048,768]{1,0:T(8,128)(2,1)}, u32[]{:S(2)}, u32[]{:S(2)}) %collective-permute-start.2) | collective-permute-done | bytes 3145760 | tf_op jit(solution)/shard_map/ppermute | solution.py:14
  136.2 4.0 fusion.107
  140.2 4.2 collective-permute-start.3
  144.4 88.6 %collective-permute-done = bf16[768,2048]{1,0:T(8,128)(2,1)} collective-permute-done((bf16[768,2048]{1,0:T(8,128)(2,1)}, bf16[768,2048]{1,0:T(8,128)(2,1)}, u32[]{:S(2)}, u32[]{:S(2)}) %collective-permute-start) | collective-permute-done | bytes 3145760 | tf_op jit(solution)/shard_map/ppermute | solution.py:14
  233.0 3.9 fusion.106
  249.1 6.1 %fusion.4 = f32[640,768]{1,0:T(8,128)} fusion(bf16[640,2048]{1,0:T(8,128)(2,1)} %bitcast.229, bf16[1,1,2048,768]{3,2,1,0:T(8,128)(2,1)} %param.12), kind=kOutput, calls=%fused_computation.23 | convolution fusion | flops 2013265920 | bytes 7733248 | tf_op jit(solution)/shard_map/dot_general | solution.py:42
  263.0 4.4 fusion.33
  275.6 31.5 %collective-permute-done.1 = bf16[768,2048]{1,0:T(8,128)(2,1)} collective-permute-done((bf16[768,2048]{1,0:T(8,128)(2,1)}, bf16[768,2048]{1,0:T(8,128)(2,1)}, u32[]{:S(2)}, u32[]{:S(2)}) %collective-permute-start.1) | collective-permute-done | bytes 3145760 | tf_op jit(solution)/shard_map/ppermute | solution.py:14
  307.2 4.9 multiply_convert_fusion.9
  316.2 4.7 pad_maximum_fusion
  320.9 7.8 %all-to-all-start.1 = ((bf16[16,50,2048]{2,1,0:T(8,128)(2,1)}), bf16[16,50,2048]{2,1,0:T(8,128)(2,1)}, u32[]{:S(2)}, u32[]{:S(2)}) async-start(bf16[16,50,2048]{2,1,0:T(8,128)(2,1)} %pad_maximum_fusion), calls=%async_computation.1 | async-start | bytes 7340032 | tf_op jit(solution)/shard_map/all_to_all | solution.py:158
  343.8 6.1 %fusion.2 = f32[640,768]{1,0:T(8,128)} fusion(bf16[640,2048]{1,0:T(8,128)(2,1)} %bitcast.235, bf16[1,1,2048,768]{3,2,1,0:T(8,128)(2,1)} %param.12), kind=kOutput, calls=%fused_computation.21 | convolution fusion | flops 2013265920 | bytes 7733248 | tf_op jit(solution)/shard_map/dot_general | solution.py:42
  358.3 5.8 %fusion.27 = (bf16[640,768]{1,0:T(8,128)(2,1)S(1)}, bf16[640,768]{1,0:T(8,128)(2,1)S(1)}, f32[640,768]{1,0:T(8,128)}) fusion(f32[16,40,768]{2,1,0:T(8,128)S(1)} %copy-done.37, f32[640,768]{1,0:T(8,128)} %fusion.2, bf16[640,2048]{1,0:T(8,128)(2,1)S(1)} %bitcast.237, bf16[1,1,768,2048]{3,2,1,0:T(8,128)(2,1)S(1)} %copy-done.2), kind=kOutput, calls=%fused_computation.53 | convolution fusion | flops 2019655680 | bytes 13631488 | tf_op jit(solution)/shard_map/dot_general | solution.py:47
  367.1 4.5 fusion.76
  376.6 5.1 multiply_convert_fusion.8
  385.7 4.4 pad_maximum_fusion.1
  390.0 8.2 %all-to-all-done.1 = bf16[16,50,2048]{2,1,0:T(8,128)(2,1)} async-done(((bf16[16,50,2048]{2,1,0:T(8,128)(2,1)}), bf16[16,50,2048]{2,1,0:T(8,128)(2,1)}, u32[]{:S(2)}, u32[]{:S(2)}) %all-to-all-start.1) | async-done | bytes 3276832 | tf_op jit(solution)/shard_map/all_to_all | solution.py:158
  398.2 17.3 %all-to-all-start.3 = ((bf16[16,50,2048]{2,1,0:T(8,128)(2,1)}), bf16[16,50,2048]{2,1,0:T(8,128)(2,1)}, u32[]{:S(2)}, u32[]{:S(2)}) async-start(bf16[16,50,2048]{2,1,0:T(8,128)(2,1)} %pad_maximum_fusion.1), calls=%async_computation.3 | async-start | bytes 7340032 | tf_op jit(solution)/shard_map/all_to_all | solution.py:158
  415.5 6.2 %fusion.12 = bf16[1,1,2048,768]{2,3,1,0:T(8,128)(2,1)} fusion(f32[768,2048]{1,0:T(8,128)} %fusion.76, bf16[640,768]{1,0:T(8,128)(2,1)} %copy-done.52, bf16[640,2048]{1,0:T(8,128)(2,1)S(1)} %bitcast.236), kind=kOutput, calls=%fused_computation.34 | convolution fusion | flops 2016411648 | bytes 13041664 | tf_op jit(solution)/shard_map/dot_general | solution.py:60
  421.7 4.8 copy.66
  426.5 4.9 fusion.40
  443.0 4.1 fusion.13
  451.7 41.0 %collective-permute-done.5 = bf16[1024,768]{0,1:T(8,128)(2,1)} collective-permute-done((bf16[1024,768]{0,1:T(8,128)(2,1)}, bf16[1024,768]{0,1:T(8,128)(2,1)}, u32[]{:S(2)}, u32[]{:S(2)}) %collective-permute-start.5) | collective-permute-done | bytes 1572896 | tf_op jit(solution)/shard_map/ppermute | solution.py:14
  497.0 29.1 %collective-permute-done.7 = bf16[384,2048]{1,0:T(8,128)(2,1)} collective-permute-done((bf16[384,2048]{1,0:T(8,128)(2,1)}, bf16[384,2048]{1,0:T(8,128)(2,1)}, u32[]{:S(2)}, u32[]{:S(2)}) %collective-permute-start.7) | collective-permute-done | bytes 1572896 | tf_op jit(solution)/shard_map/ppermute | solution.py:14
  555.9 10.8 %collective-permute-done.8 = f32[192,2048]{1,0:T(8,128)} collective-permute-done((f32[192,2048]{1,0:T(8,128)}, f32[192,2048]{1,0:T(8,128)}, u32[]{:S(2)}, u32[]{:S(2)}) %collective-permute-start.8) | collective-permute-done | bytes 1572896 | tf_op jit(solution)/shard_map/ppermute | solution.py:14
  (221 shorter events, 146.3 us)
Async XLA Ops:
  16.9 8.7 %copy-start.49 = (s32[1,4]{1,0:T(1,128)S(1)}, s32[1,4]{1,0:T(1,128)}, u32[]{:S(2)}) copy-start(s32[1,4]{1,0:T(1,128)} %param.11) | copy-start | bytes 52
  16.9 10.0 %copy-start.3 = (bf16[1,1,2048,768]{3,2,1,0:T(8,128)(2,1)S(1)}, bf16[1,1,2048,768]{3,2,1,0:T(8,128)(2,1)}, u32[]{:S(2)}) copy-start(bf16[1,1,2048,768]{3,2,1,0:T(8,128)(2,1)} %param.12) | copy-start | bytes 9437188
  16.9 78.8 %all-to-all-start = ((bf16[16,50,2048]{2,1,0:T(8,128)(2,1)}), bf16[16,50,2048]{2,1,0:T(8,128)(2,1)}, u32[]{:S(2)}, u32[]{:S(2)}) async-start(bf16[16,50,2048]{2,1,0:T(8,128)(2,1)} %reshape.671), calls=%async_computation | async-start | bytes 7340032 | tf_op jit(solution)/shard_map/all_to_all | solution.py:118
  28.8 107.4 %collective-permute-start.2 = (bf16[2048,768]{1,0:T(8,128)(2,1)}, bf16[2048,768]{1,0:T(8,128)(2,1)}, u32[]{:S(2)}, u32[]{:S(2)}) collective-permute-start(bf16[2048,768]{1,0:T(8,128)(2,1)} %bitcast_multiply_fusion.2), channel_id=1, source_target_pairs={{0,1},{1,0},{2,3},{3,2},{4,5},{5,4},{6,7},{7,6},{8,9},{9,8},{10,11... | collective-permute-start | bytes 9437192 | tf_op jit(solution)/shard_map/ppermute | solution.py:14
  32.5 200.5 %collective-permute-start = (bf16[768,2048]{1,0:T(8,128)(2,1)}, bf16[768,2048]{1,0:T(8,128)(2,1)}, u32[]{:S(2)}, u32[]{:S(2)}) collective-permute-start(bf16[768,2048]{1,0:T(8,128)(2,1)} %bitcast_multiply_fusion.3), channel_id=1, source_target_pairs={{0,1},{1,0},{2,3},{3,2},{4,5},{5,4},{6,7},{7,6},{8,9},{9,8},{10,11... | collective-permute-start | bytes 9437192 | tf_op jit(solution)/shard_map/ppermute | solution.py:14
  95.7 225.1 %all-to-all-start.2 = ((bf16[16,50,2048]{2,1,0:T(8,128)(2,1)}), bf16[16,50,2048]{2,1,0:T(8,128)(2,1)}, u32[]{:S(2)}, u32[]{:S(2)}) async-start(bf16[16,50,2048]{2,1,0:T(8,128)(2,1)} %reshape.678), calls=%async_computation.2 | async-start | bytes 7340032 | tf_op jit(solution)/shard_map/all_to_all | solution.py:118
  122.2 14.0 %copy-start.4 = (bf16[1,1,2048,768]{3,2,1,0:T(8,128)(2,1)S(1)}, bf16[1,1,2048,768]{3,2,1,0:T(8,128)(2,1)}, u32[]{:S(2)}) copy-start(bf16[1,1,2048,768]{3,2,1,0:T(8,128)(2,1)} %param.12) | copy-start | bytes 9437188
  123.8 109.1 %copy-start.1 = (bf16[1,1,768,2048]{3,2,1,0:T(8,128)(2,1)S(1)}, bf16[1,1,768,2048]{3,2,1,0:T(8,128)(2,1)}, u32[]{:S(2)}) copy-start(bf16[1,1,768,2048]{3,2,1,0:T(8,128)(2,1)} %param.13) | copy-start | bytes 9437188
  140.2 99.9 %copy-start.34 = (bf16[1,2,1,16,50,768]{5,3,4,2,1,0:T(8,128)(2,1)S(1)}, bf16[1,2,1,16,50,768]{5,3,4,2,1,0:T(8,128)(2,1)}, u32[]{:S(2)}) copy-start(bf16[1,2,1,16,50,768]{5,3,4,2,1,0:T(8,128)(2,1)} %param.15) | copy-start | bytes 7372804
  140.2 131.0 %collective-permute-start.3 = (bf16[2048,768]{1,0:T(8,128)(2,1)}, bf16[2048,768]{1,0:T(8,128)(2,1)}, u32[]{:S(2)}, u32[]{:S(2)}) collective-permute-start(bf16[2048,768]{1,0:T(8,128)(2,1)} %fusion.107), channel_id=1, source_target_pairs={{0,2},{1,3},{2,0},{3,1},{4,6},{5,7},{6,4},{7,5},{8,10},{9,11},{10,... | collective-permute-start | bytes 9437192 | tf_op jit(solution)/shard_map/ppermute | solution.py:14
  236.8 70.3 %collective-permute-start.1 = (bf16[768,2048]{1,0:T(8,128)(2,1)}, bf16[768,2048]{1,0:T(8,128)(2,1)}, u32[]{:S(2)}, u32[]{:S(2)}) collective-permute-start(bf16[768,2048]{1,0:T(8,128)(2,1)} %fusion.106), channel_id=1, source_target_pairs={{0,2},{1,3},{2,0},{3,1},{4,6},{5,7},{6,4},{7,5},{8,10},{9,11},{10,... | collective-permute-start | bytes 9437192 | tf_op jit(solution)/shard_map/ppermute | solution.py:14
  262.2 5.2 copy-start.14
  274.9 32.3 %copy-start.23 = (f32[160,768]{1,0:T(8,128)S(1)}, f32[160,768]{1,0:T(8,128)}, u32[]{:S(2)}) copy-start(f32[160,768]{1,0:T(8,128)} %reshape.694) | copy-start | bytes 1474564
  274.9 32.3 %copy-start.27 = (bf16[160,2048]{1,0:T(8,128)(2,1)S(1)}, bf16[160,2048]{1,0:T(8,128)(2,1)}, u32[]{:S(2)}) copy-start(bf16[160,2048]{1,0:T(8,128)(2,1)} %reshape.674) | copy-start | bytes 1966084
  275.6 36.5 %copy-start.25 = (f32[160,768]{1,0:T(8,128)}, f32[160,768]{1,0:T(8,128)S(1)}, u32[]{:S(2)}) copy-start(f32[160,768]{1,0:T(8,128)S(1)} %convolution_bitcast_fusion.1) | copy-start | bytes 1474564
  320.9 77.3 %all-to-all-start.1 = ((bf16[16,50,2048]{2,1,0:T(8,128)(2,1)}), bf16[16,50,2048]{2,1,0:T(8,128)(2,1)}, u32[]{:S(2)}, u32[]{:S(2)}) async-start(bf16[16,50,2048]{2,1,0:T(8,128)(2,1)} %pad_maximum_fusion), calls=%async_computation.1 | async-start | bytes 7340032 | tf_op jit(solution)/shard_map/all_to_all | solution.py:158
  356.5 7.5 %copy-start.30 = (bf16[16,40,2048]{2,1,0:T(8,128)(2,1)}, bf16[16,40,2048]{2,1,0:T(8,128)(2,1)S(1)}, u32[]{:S(2)}) copy-start(bf16[16,40,2048]{2,1,0:T(8,128)(2,1)S(1)} %slice.116) | copy-start | bytes 7864324
  358.3 7.0 %copy-start.46 = (bf16[640,768]{1,0:T(8,128)(2,1)S(1)}, bf16[640,768]{1,0:T(8,128)(2,1)}, u32[]{:S(2)}) copy-start(bf16[640,768]{1,0:T(8,128)(2,1)} %get-tuple-element.28) | copy-start | bytes 2949124
  364.1 7.6 %copy-start.52 = (bf16[640,768]{1,0:T(8,128)(2,1)}, bf16[640,768]{1,0:T(8,128)(2,1)S(1)}, u32[]{:S(2)}) copy-start(bf16[640,768]{1,0:T(8,128)(2,1)S(1)} %get-tuple-element.31) | copy-start | bytes 2949124
  376.6 5.1 copy-start.42
  390.0 25.5 %copy-start.29 = (bf16[16,40,2048]{2,1,0:T(8,128)(2,1)S(1)}, bf16[16,40,2048]{2,1,0:T(8,128)(2,1)}, u32[]{:S(2)}) copy-start(bf16[16,40,2048]{2,1,0:T(8,128)(2,1)} %slice.121) | copy-start | bytes 7864324
  398.2 140.5 %all-to-all-start.3 = ((bf16[16,50,2048]{2,1,0:T(8,128)(2,1)}), bf16[16,50,2048]{2,1,0:T(8,128)(2,1)}, u32[]{:S(2)}, u32[]{:S(2)}) async-start(bf16[16,50,2048]{2,1,0:T(8,128)(2,1)} %pad_maximum_fusion.1), calls=%async_computation.3 | async-start | bytes 7340032 | tf_op jit(solution)/shard_map/all_to_all | solution.py:158
  421.7 4.8 copy-start.15
  426.5 4.9 copy-start.18
  434.9 57.7 %collective-permute-start.5 = (bf16[1024,768]{0,1:T(8,128)(2,1)}, bf16[1024,768]{0,1:T(8,128)(2,1)}, u32[]{:S(2)}, u32[]{:S(2)}) collective-permute-start(bf16[1024,768]{0,1:T(8,128)(2,1)} %dynamic-slice_bitcast_fusion), channel_id=1, source_target_pairs={{0,2},{1,3},{2,0},{3,1},{4,6},{5,7},{6,4},{7,5},{8,10},{9,11},{10,... | collective-permute-start | bytes 4718600 | tf_op jit(solution)/shard_map/ppermute | solution.py:14
  442.1 84.0 %collective-permute-start.7 = (bf16[384,2048]{1,0:T(8,128)(2,1)}, bf16[384,2048]{1,0:T(8,128)(2,1)}, u32[]{:S(2)}, u32[]{:S(2)}) collective-permute-start(bf16[384,2048]{1,0:T(8,128)(2,1)} %constant_dynamic-slice_fusion.1), channel_id=1, source_target_pairs={{0,2},{1,3},{2,0},{3,1},{4,6},{5,7},{6,4},{7,5},{8,10},{9,11},{10,... | collective-permute-start | bytes 4718600 | tf_op jit(solution)/shard_map/ppermute | solution.py:14
  494.7 33.4 %copy-start.7 = (f32[1024,768]{0,1:T(8,128)}, f32[1024,768]{0,1:T(8,128)S(1)}, u32[]{:S(2)}) copy-start(f32[1024,768]{0,1:T(8,128)S(1)} %bitcast_add_fusion) | copy-start | bytes 9437188
  494.7 31.4 %copy-start.12 = (bf16[768,2048]{1,0:T(8,128)(2,1)S(1)}, bf16[768,2048]{1,0:T(8,128)(2,1)}, u32[]{:S(2)}) copy-start(bf16[768,2048]{1,0:T(8,128)(2,1)} %copy-done.11) | copy-start | bytes 9437188
  496.0 54.8 %collective-permute-start.6 = (f32[512,768]{0,1:T(8,128)}, f32[512,768]{0,1:T(8,128)}, u32[]{:S(2)}, u32[]{:S(2)}) collective-permute-start(f32[512,768]{0,1:T(8,128)} %constant_dynamic-slice_fusion.2), channel_id=1, source_target_pairs={{0,1},{1,0},{2,3},{3,2},{4,5},{5,4},{6,7},{7,6},{8,9},{9,8},{10,11... | collective-permute-start | bytes 4718600 | tf_op jit(solution)/shard_map/ppermute | solution.py:14
  530.3 36.5 %collective-permute-start.8 = (f32[192,2048]{1,0:T(8,128)}, f32[192,2048]{1,0:T(8,128)}, u32[]{:S(2)}, u32[]{:S(2)}) collective-permute-start(f32[192,2048]{1,0:T(8,128)} %constant_dynamic-slice_fusion), channel_id=1, source_target_pairs={{0,1},{1,0},{2,3},{3,2},{4,5},{5,4},{6,7},{7,6},{8,9},{9,8},{10,11... | collective-permute-start | bytes 4718600 | tf_op jit(solution)/shard_map/ppermute | solution.py:14
  549.9 16.8 %copy-start.10 = (f32[384,2048]{1,0:T(8,128)S(1)}, f32[384,2048]{1,0:T(8,128)}, u32[]{:S(2)}) copy-start(f32[384,2048]{1,0:T(8,128)} %copy-done.9) | copy-start | bytes 9437188
  550.8 18.4 %collective-permute-start.4 = (bf16[2,64,2048]{2,1,0:T(8,128)(2,1)}, bf16[2,64,2048]{2,1,0:T(8,128)(2,1)}, u32[]{:S(2)}, u32[]{:S(2)}) collective-permute-start(bf16[2,64,2048]{2,1,0:T(8,128)(2,1)} %pad_maximum_fusion.2), channel_id=1, source_target_pairs={{16,0},{0,16},{17,1},{1,17},{18,2},{2,18},{19,3},{3,19},{20,4},{4,... | collective-permute-start | bytes 1572872 | tf_op jit(solution)/shard_map/ppermute | solution.py:20
  (34 other events, 99.7 us)
where the time goes:
time: 581 us; the launch traced here: 572 us
  waiting for transfers between devices  270 us (46%)
  local copies, waits for them, and re-layouts  103 us (18%)
  matrix products  69 us (12%)
  starting transfers between devices  65.5 us (11%)
  other arithmetic  61.7 us (11%)
    ppermute x8, waiting for transfers between devices, partner(): return lax.ppermute(value, axis, pairs)  213 us
    all_to_all x2, waiting for transfers between devices, per_device(): lax.all_to_all(buffer, 'expert', split_axis=0, concat_axis=0, tiled=True)  48.3 us
    all_to_all x2, starting transfers between devices, per_device(): lax.all_to_all(buffer, 'expert', split_axis=0, concat_axis=0, tiled=True)  26.4 us
    all_to_all x2, starting transfers between devices, per_device(): lax.all_to_all(results[0], 'expert', split_axis=0, concat_axis=0, tiled=T...  25 us
    dot_general x4, matrix products, expert_rows(): lax.dot_general(grad_rows, down_w, (((1,), (1,)), ((), ())), preferred_el...  20.1 us
    unnamed x109, local copies, waits for them, and re-layouts  16.6 us
    ppermute x8, starting transfers between devices, partner(): return lax.ppermute(value, axis, pairs)  14.1 us
    dot_general x4, matrix products, expert_rows(): up_value = jnp.dot(input_rows, up_w, preferred_element_type=jnp.float32)  13.7 us
  transfers between devices with their start and end apart: 13, of which 8 were waited for; matrix products, arithmetic and copies ran while one was open for 36% of the time, Pallas kernels for 0%

commit v1 on v0

v1 whole, which is shorter than its diff:
```python
import jax
import jax.numpy as jnp
from jax import lax
from jax.sharding import PartitionSpec as P

TOP = 8
REPL = 4
MB = 2
BF16 = jnp.bfloat16
F32 = jnp.float32


def partner(value, axis, bit):
    mask = 2**bit
    pairs = [(source, source ^ mask) for source in range(lax.axis_size(axis))]
    return lax.ppermute(value, axis, pairs)


def from_behind(block, axis, distance):
    devices = range(lax.axis_size(axis))
    route = [((i - distance) % len(devices), i) for i in devices]
    return lax.ppermute(block, axis, route)


def pick(array, index, axis):
    return lax.dynamic_index_in_dim(array, index, axis, keepdims=False)


def dot_nn(a, b):
    return jnp.dot(a, b, preferred_element_type=F32)


def dot_nt(a, b):
    return lax.dot_general(a, b, (((1,), (1,)), ((), ())), preferred_element_type=F32)


def dot_tn(a, b):
    return lax.dot_general(a, b, (((0,), (0,)), ((), ())), preferred_element_type=F32)


def gate_parts(gates):
    value = gates.astype(F32)
    sig = jax.nn.sigmoid(value)
    return value * sig, sig * (1.0 + value * (1.0 - sig))


def per_device(
    grad_out, route_weights, expert_ids, hot_pos, up_weight, down_weight, saved_inputs, saved_gates
):
    experts = lax.axis_size("expert")
    device = lax.axis_index("expert")
    features = grad_out.shape[-1]
    hidden_units = saved_gates.shape[-1]
    tokens = grad_out.shape[2]
    slots = saved_inputs.shape[4]
    quarter_rows = slots // (REPL + 1)
    most = REPL * quarter_rows
    quarter = hidden_units // REPL
    groups = [[REPL * g + j for j in range(REPL)] for g in range(experts // REPL)]
    hot_table = hot_pos[0]
    group_id = device // REPL
    local_pos = device % REPL
    low_bit = local_pos % 2
    high_bit = local_pos // 2
    owner_pos = jnp.sum(
        jnp.where(jnp.arange(hot_table.shape[0], dtype=jnp.int32) == group_id, hot_table, 0)
    )
    is_owner = local_pos == owner_pos
    hot_expert = REPL * group_id + owner_pos

    meta = jnp.concatenate([expert_ids[0].astype(F32), route_weights[0]], -1)
    meta = lax.all_gather(meta, "expert", axis=1)
    grads = [lax.all_gather(grad_out[0, b], "expert", axis=0, tiled=True) for b in range(MB)]

    own_up = up_weight[0, 0]
    own_down = down_weight[0, 0]
    owner_mask = is_owner.astype(BF16)
    up_t = (own_up.T * owner_mask).reshape(2, 2, quarter, features)
    down = (own_down * owner_mask).reshape(2, 2, quarter, features)
    up_in = partner(pick(up_t, 1 - low_bit, 1), "expert", 0)
    down_in = partner(pick(down, 1 - high_bit, 0), "expert", 1)
    up_half = pick(up_t, low_bit, 1) + up_in
    down_half = pick(down, high_bit, 0) + down_in
    up_in = partner(pick(up_half, 1 - high_bit, 0), "expert", 1)
    down_in = partner(pick(down_half, 1 - low_bit, 0), "expert", 0)
    hot_up = pick(up_half, high_bit, 0) + up_in
    hot_down = pick(down_half, low_bit, 0) + down_in

    inputs = saved_inputs[0, :, 0]
    gates = saved_gates[0, :, 0]
    hot_rows = experts * quarter_rows
    hot_inputs = inputs[:, :, most:].reshape(MB * hot_rows, features)
    hot_inputs = lax.all_gather(hot_inputs, "expert", axis=0, axis_index_groups=groups)
    hot_inputs = hot_inputs.reshape(REPL, MB, hot_rows, features)
    hot_gates = gates[:, :, most:].reshape(MB * hot_rows, REPL, quarter).transpose(1, 0, 2)
    hot_gates = lax.all_to_all(hot_gates, "expert", 0, 0, axis_index_groups=groups, tiled=True)
    hot_gates = hot_gates.reshape(REPL, MB, hot_rows, quarter)

    ids = meta[..., :TOP]
    weights = meta[..., TOP:]
    own_hit = (ids == device.astype(F32)) & jnp.logical_not(is_owner)
    hot_hit = ids == hot_expert.astype(F32)
    own_weight = jnp.sum(jnp.where(own_hit, weights, 0.0), -1)
    hot_weight = jnp.sum(jnp.where(hot_hit, weights, 0.0), -1)
    own_named = jnp.any(own_hit, -1)
    hot_named = jnp.any(hot_hit, -1)
    own_place = jnp.where(own_named, jnp.cumsum(own_named.astype(jnp.int32), -1) - 1, -1)
    hot_place = jnp.where(hot_named, jnp.cumsum(hot_named.astype(jnp.int32), -1) - 1, -1)
    own_select = (own_place[..., None] == jnp.arange(slots, dtype=jnp.int32)).astype(BF16)
    block = jnp.arange(experts, dtype=jnp.int32)
    replica = jnp.arange(REPL, dtype=jnp.int32)
    order = (
        REPL * jnp.arange(quarter_rows, dtype=jnp.int32)[None, None, :]
        + (replica[:, None, None] - block[None, :, None]) % REPL
    )
    same = block[:, None, None, None, None] == block[None, None, None, :, None]
    hot_select = [
        ((hot_place[b][:, :, None, None, None] == order[None, None]) & same)
        .astype(BF16)
        .reshape(experts * tokens, REPL * hot_rows)
        for b in range(MB)
    ]

    parts = []
    returned = []
    gate_grads = []
    hot_gate_grads = []
    for b in range(MB):
        own_x = jnp.einsum(
            "etc,ecd->etd", own_select[b], inputs[b], preferred_element_type=F32
        ).astype(BF16).reshape(experts * tokens, features)
        own_a = jnp.einsum(
            "etc,ecd->etd", own_select[b], gates[b], preferred_element_type=F32
        ).astype(BF16).reshape(experts * tokens, hidden_units)
        hot_x = dot_nn(
            hot_select[b], hot_inputs[:, b].reshape(REPL * hot_rows, features)
        ).astype(BF16)
        hot_a = dot_nn(
            hot_select[b], hot_gates[:, b].reshape(REPL * hot_rows, quarter)
        ).astype(BF16)
        grad = grads[b].astype(F32)
        own_g = (own_weight[b].reshape(-1, 1) * grad).astype(BF16)
        hot_g = (hot_weight[b].reshape(-1, 1) * grad).astype(BF16)
        own_act, own_slope = gate_parts(own_a)
        hot_act, hot_slope = gate_parts(hot_a)
        own_uv = dot_nn(own_x, own_up)
        hot_uv = dot_nt(hot_x, hot_up)
        own_gh = dot_nt(own_g, own_down)
        hot_gh = dot_nt(hot_g, hot_down)
        own_gu = (own_gh * own_act).astype(BF16)
        hot_gu = (hot_gh * hot_act).astype(BF16)
        own_hidden = (own_act * own_uv).astype(BF16)
        hot_hidden = (hot_act * hot_uv).astype(BF16)
        own_gg = (own_gh * own_uv * own_slope).astype(BF16)
        hot_gg = (hot_gh * hot_uv * hot_slope).astype(BF16)
        term = (dot_nt(own_gu, own_up) + dot_nn(hot_gu, hot_up)).astype(BF16)
        returned.append(
            lax.psum_scatter(term.reshape(experts, tokens, features), "expert")
        )
        gate_grads.append(
            jnp.einsum(
                "etc,etf->ecf",
                own_select[b],
                own_gg.reshape(experts, tokens, hidden_units),
                preferred_element_type=F32,
            ).astype(BF16)
        )
        hot_gate_grads.append(
            dot_tn(hot_select[b], hot_gg).astype(BF16).reshape(REPL, hot_rows, quarter)
        )
        parts.append((own_x, own_gu, own_hidden, own_g, hot_x, hot_gu, hot_hidden, hot_g))
    own_x, own_gu, own_hidden, own_g, hot_x, hot_gu, hot_hidden, hot_g = (
        [member[n] for member in parts] for n in range(8)
    )
    hot_up_grad = sum(dot_tn(hot_gu[b], hot_x[b]) for b in range(MB)).astype(BF16)
    hot_down_grad = sum(dot_tn(hot_hidden[b], hot_g[b]) for b in range(MB)).astype(BF16)
    up_grad = sum(dot_tn(own_x[b], own_gu[b]) for b in range(MB)).astype(BF16)
    down_grad = sum(dot_tn(own_hidden[b], own_g[b]) for b in range(MB)).astype(BF16)

    hot_up_grad = lax.all_to_all(
        hot_up_grad, "expert", 1, 0, axis_index_groups=groups, tiled=True
    ).T
    back = jnp.stack(hot_gate_grads, 1).reshape(REPL, MB * hot_rows, quarter)
    back = lax.all_to_all(back, "expert", 0, 0, axis_index_groups=groups, tiled=True)
    back = back.transpose(1, 0, 2).reshape(MB, experts, quarter_rows, hidden_units)
    gate_grad = jnp.concatenate([jnp.stack(gate_grads, 0)[:, :, :most], back], 2)

    token_grads = jnp.stack(
        [
            (returned[b].astype(F32) + grad_out[0, b].astype(F32)).astype(BF16)
            for b in range(MB)
        ],
        0,
    )
    sent_back = from_behind(token_grads, "pipe", -1)
    return (
        sent_back[None],
        up_grad[None, None],
        down_grad[None, None],
        gate_grad[None, :, None],
        hot_up_grad[None, None],
        hot_down_grad[None, None],
    )


def solution(mesh):
    return jax.shard_map(
        per_device,
        mesh=mesh,
        in_specs=(
            P("pipe", None, "expert", None),
            P("pipe", None, "expert", None),
            P("pipe", None, "expert", None),
            P("pipe", None),
            P("pipe", "expert", None, None),
            P("pipe", "expert", None, None),
            P("pipe", None, "expert", None, None, None),
            P("pipe", None, "expert", None, None, None),
        ),
        out_specs=(
            P("pipe", None, "expert", None),
            P("pipe", "expert", None, None),
            P("pipe", "expert", None, None),
            P("pipe", None, "expert", None, None, None),
            P("pipe", "expert", None, None),
            P("pipe", "expert", None, None),
        ),
        check_vma=False,
    )
```

time: 581 us -> 497 us (0.86)
  waiting for transfers between devices: 270 us -> 123 us
  blocking collectives: 0 us -> 84.4 us
  matrix products: 69 us -> 120 us
  starting transfers between devices: 65.5 us -> 17.5 us
  local copies, waits for them, and re-layouts: 103 us -> 78.8 us
  between operations: 2.46 us -> 16.2 us
  other arithmetic: 61.7 us -> 51.6 us
    ppermute x8 -> x4, waiting for transfers between devices: 213 us -> 22.4 us  [partner(): return lax.ppermute(value, axis, pairs)]
    reduce_scatter x0 -> x2, waiting for transfers between devices: none -> 98.6 us  [per_device(): lax.psum_scatter(term.reshape(experts, tokens, features), 'expert')]
    all_gather x0 -> x1, blocking collectives: none -> 84.4 us  [per_device(): meta = lax.all_gather(meta, 'expert', axis=1)]
    all_to_all x4 -> x3, waiting for transfers between devices: 56.6 us -> 1.28 us  [the longest x1 1.28 us: per_device(): lax.all_to_all(hot_up_grad, 'expert', 1, 0, axis_index_groups=groups, til...]
    dot_general x20 -> x32, matrix products: 69 us -> 120 us  [the longest x8 36.9 us: dot_nt(): lax.dot_general(a, b, (((1,), (1,)), ((), ())), preferred_element_type=F32)]
    all_to_all x4 -> x3, starting transfers between devices: 51.5 us -> 13.2 us  [the longest x1 5.16 us: per_device(): lax.all_to_all(hot_gates, 'expert', 0, 0, axis_index_groups=groups, tiled...]
    reduce_or x0 -> x1, other arithmetic: none -> 35.8 us  [per_device(): own_named = jnp.any(own_hit, -1)]
    reshape x16 -> x3, local copies, waits for them, and re-layouts: 29.3 us -> 5.91 us  [the longest x1 2.83 us: per_device(): gates[:, :, most:].reshape(MB * hot_rows, REPL, quarter).transpose(1, 0, 2)]
  transfers between devices with their start and end apart: 13 -> 13, of which waited for: 8 -> 5; matrix products, arithmetic and copies ran while one was open for 36% -> 48% of each run, Pallas kernels for 0% -> 0%
where the time goes in v1:
time: 497 us; the launch traced here: 492 us
  waiting for transfers between devices  123 us (25%)
  matrix products  120 us (24%)
  blocking collectives  84.4 us (17%)
  local copies, waits for them, and re-layouts  78.8 us (16%)
  other arithmetic  51.6 us (10%)
  starting transfers between devices  17.5 us (4%)
  between operations  16.2 us (3%)
    reduce_scatter x2, waiting for transfers between devices, per_device(): lax.psum_scatter(term.reshape(experts, tokens, features), 'expert')  98.6 us
    all_gather x1, blocking collectives, per_device(): meta = lax.all_gather(meta, 'expert', axis=1)  84.4 us
    dot_general x8, matrix products, dot_nt(): lax.dot_general(a, b, (((1,), (1,)), ((), ())), preferred_element_type=F32)  36.9 us
    reduce_or x1, other arithmetic, per_device(): own_named = jnp.any(own_hit, -1)  35.8 us
    dot_general x10, matrix products, dot_tn(): lax.dot_general(a, b, (((0,), (0,)), ((), ())), preferred_element_type=F32)  32.2 us
    dot_general x8, matrix products, dot_nn(): return jnp.dot(a, b, preferred_element_type=F32)  29.1 us
    ppermute x4, waiting for transfers between devices, partner(): return lax.ppermute(value, axis, pairs)  22.4 us
    unnamed x126, local copies, waits for them, and re-layouts  21.9 us
  transfers between devices with their start and end apart: 13, of which 5 were waited for; matrix products, arithmetic and copies ran while one was open for 48% of the time, Pallas kernels for 0%

profile of v1, /device:TPU:0, one launch (start us, length us, event | category | flops | bytes accessed | tf_op | source)
XLA Modules:
  0.0 491.5 jit_solution(4409726872215106232)
XLA Ops:
  17.1 5.2 %all-to-all-start = ((bf16[4,320,192]{1,2,0:T(8,128)(2,1)}), bf16[4,320,192]{1,2,0:T(8,128)(2,1)}, u32[]{:S(2)}, u32[]{:S(2)}) async-start(bf16[4,320,192]{1,2,0:T(8,128)(2,1)} %copy.142), calls=%async_computation | async-start | bytes 1179648 | tf_op jit(solution)/shard_map/all_to_all | solution.py:96
  40.4 6.8 %fusion.88 = (bf16[1,1,1,16,50,2048]{5,3,4,2,1,0:T(8,128)(2,1)}, bf16[1,1,1,16,50,2048]{5,3,4,2,1,0:T(8,128)(2,1)}) fusion(bf16[1,2,1,16,50,2048]{5,3,4,2,1,0:T(8,128)(2,1)} %param.14), kind=kLoop, calls=%fused_computation.158 | loop fusion | bytes 13107200 | tf_op jit(solution)/shard_map/slice | solution.py:130
  48.0 84.4 %all-gather = f32[2,1024,16]{2,0,1:T(2,128)S(1)} all-gather(f32[2,64,16]{2,0,1:T(2,128)S(1)} %copy.134), channel_id=2, replica_groups=mesh['pipe'=2,'expert'=16] {'expert'}, dimensions={1}, use_global_device_ids=true | all-gather | bytes 139264 | tf_op jit(solution)/shard_map/all_gather | solution.py:72
  132.4 35.8 %fusion.87 = (pred[2,16,64]{0,2,1:T(8,128)(4,1)S(1)}, pred[2,16,64,8]{3,0,2,1:T(4,128)(4,1)S(1)}, pred[2,16,64]{0,2,1:T(8,128)(4,1)S(1)}) fusion(pred[]{:T(512)S(6)} %not.3, f32[]{:T(128)S(6)} %convert_element_type.198, f32[2,16,64,16]{3,0,2,1:T(2,128)S(1)} %bitcast.210, f32[]{:T(128)S(6)} %convert_element_type.206), kind=kLoop, calls=%fused_computation.157 | loop fusion | flops 77824 | bytes 86025 | tf_op jit(solution)/shard_map/reduce_or | solution.py:105
  169.7 6.8 %convolution_convert_fusion.3 = bf16[16,64,2048]{2,1,0:T(8,128)(2,1)S(1)} fusion(bf16[1,1,1,16,50,2048]{5,3,4,2,1,0:T(8,128)(2,1)} %get-tuple-element.63, pred[2,16,64,50]{2,3,1,0:T(8,128)(4,1)S(1)} %iota_compare_fusion.1), kind=kOutput, calls=%fused_computation.26 | convolution fusion | flops 211812352 | bytes 7585792 | tf_op jit(solution)/shard_map/etc,ecd->etd/dot_general | solution.py:129
  176.5 5.1 %fusion.22 = f32[1024,768]{1,0:T(8,128)} fusion(bf16[1024,2048]{1,0:T(8,128)(2,1)S(1)} %bitcast.218, bf16[1,1,2048,768]{3,2,1,0:T(8,128)(2,1)S(1)} %copy-done.18), kind=kOutput, calls=%fused_computation.45 | convolution fusion | flops 3221225472 | bytes 10485760 | tf_op jit(solution)/shard_map/dot_general | solution.py:30
  181.7 3.7 compare_and_fusion.1
  185.4 3.7 select_reduce_fusion
  191.8 4.8 and.109
  209.7 20.1 %collective-permute-done.3 = bf16[192,2048]{1,0:T(8,128)(2,1)S(1)} collective-permute-done((bf16[192,2048]{1,0:T(8,128)(2,1)S(1)}, bf16[192,2048]{1,0:T(8,128)(2,1)S(1)}, u32[]{:S(2)}, u32[]{:S(2)}) %collective-permute-start.3) | collective-permute-done | bytes 786464 | tf_op jit(solution)/shard_map/ppermute | solution.py:16
  232.1 6.2 %multiply_convert_fusion.11 = (bf16[1024,192]{0,1:T(8,128)(2,1)S(1)}, f32[1024,192]{0,1:T(8,128)}) fusion(f32[1024,192]{0,1:T(8,128)} %fusion.64, bf16[192,2048]{1,0:T(8,128)(2,1)} %collective-permute-done.1, bf16[2,192,2048]{2,1,0:T(8,128)(2,1)S(1)} %bitcast_add_fusion.1, s32[]{:T(128)S(6)} %select_n.86, ...), kind=kOutput, calls=%fused_computation.119 | convolution fusion | flops 813170688 | bytes 7737348 | tf_op jit(solution)/shard_map/dot_general | solution.py:34
  239.5 6.4 %fusion.12 = (bf16[1024,768]{1,0:T(8,128)(2,1)}, bf16[1024,768]{1,0:T(8,128)(2,1)S(1)}, f32[1024,768]{1,0:T(8,128)}) fusion(f32[1024,768]{1,0:T(8,128)S(1)} %copy-done.49, bf16[16,64,768]{2,1,0:T(8,128)(2,1)S(1)} %copy-done.29, bf16[1,1,768,2048]{3,2,1,0:T(8,128)(2,1)S(1)} %copy-done.16, bf16[1,1,1024,2048]{3,2,1,0:T(8,128)(2,1)S(1)} %copy-done.41, ...), kind=kOutput, calls=%fused_computation.35 | convolution fusion | flops 3238526976 | bytes 18354176 | tf_op jit(solution)/shard_map/dot_general | solution.py:34
  245.9 3.4 fusion.26
  254.7 4.8 and.112
  259.6 4.7 and.111
  267.5 4.8 convolution_convert_fusion.2
  272.4 5.1 %fusion.20 = f32[1024,768]{1,0:T(8,128)} fusion(bf16[1024,2048]{1,0:T(8,128)(2,1)S(1)} %bitcast.220, bf16[1,1,2048,768]{3,2,1,0:T(8,128)(2,1)S(1)} %copy-done.20), kind=kOutput, calls=%fused_computation.43 | convolution fusion | flops 3221225472 | bytes 10485760 | tf_op jit(solution)/shard_map/dot_general | solution.py:30
  278.9 5.4 %multiply_convert_fusion.10 = (bf16[1024,192]{0,1:T(8,128)(2,1)S(1)}, f32[1024,192]{0,1:T(8,128)}) fusion(f32[1024,192]{0,1:T(8,128)} %fusion.65, bf16[192,2048]{1,0:T(8,128)(2,1)} %collective-permute-done.1, bf16[2,192,2048]{2,1,0:T(8,128)(2,1)S(1)} %copy-done.13, s32[]{:T(128)S(6)} %select_n.86, ...), kind=kOutput, calls=%fused_computation.115 | convolution fusion | flops 813170688 | bytes 7737348 | tf_op jit(solution)/shard_map/dot_general | solution.py:34
  285.6 6.6 %fusion.19 = (bf16[1024,768]{1,0:T(8,128)(2,1)}, bf16[1024,768]{1,0:T(8,128)(2,1)S(1)}, f32[1024,768]{1,0:T(8,128)}) fusion(f32[1024,768]{1,0:T(8,128)S(1)} %copy-done.54, bf16[16,64,768]{2,1,0:T(8,128)(2,1)S(1)} %copy-done.30, bf16[1,1,768,2048]{3,2,1,0:T(8,128)(2,1)S(1)} %copy-done.17, bf16[1,1,1024,2048]{3,2,1,0:T(8,128)(2,1)S(1)} %copy-done.43, ...), kind=kOutput, calls=%fused_computation.42 | convolution fusion | flops 3238526976 | bytes 18354176 | tf_op jit(solution)/shard_map/dot_general | solution.py:34
  292.2 3.4 fusion.24
  299.0 5.7 %fusion.89 = (bf16[4,1,160,2048]{3,2,1,0:T(8,128)(2,1)}, bf16[4,1,160,2048]{3,2,1,0:T(8,128)(2,1)}) fusion(bf16[4,2,160,2048]{3,2,1,0:T(8,128)(2,1)} %bitcast.217), kind=kLoop, calls=%fused_computation.159 | loop fusion | bytes 10485760 | tf_op jit(solution)/shard_map/slice | solution.py:136
  305.8 5.5 %convolution_convert_fusion.1 = bf16[1024,2048]{1,0:T(8,128)(2,1)S(1)} fusion(pred[1024,640]{0,1:T(32,128)(4,1)S(1)} %copy-done.24, bf16[640,2048]{1,0:T(8,128)(2,1)} %bitcast.225), kind=kOutput, calls=%fused_computation.24 | convolution fusion | flops 2686451712 | bytes 7471104 | tf_op jit(solution)/shard_map/dot_general | solution.py:30
  314.7 3.8 convolution_convert_fusion
  323.4 3.9 fusion.95
  330.8 3.7 all-to-all-start.1
  336.4 3.8 fusion.54
  343.6 5.5 %fusion.94 = f32[2048,768]{1,0:T(8,128)} fusion(bf16[1024,2048]{1,0:T(8,128)(2,1)S(1)} %bitcast.219, bf16[1024,768]{1,0:T(8,128)(2,1)S(1)} %copy-done.58), kind=kOutput, calls=%fused_computation.164 | convolution fusion | flops 3221225472 | bytes 12058624 | tf_op jit(solution)/shard_map/dot_general | solution.py:38
  349.6 3.9 fusion.48
  353.6 7.0 %fusion.32 = bf16[1,1,2048,768]{3,2,1,0:T(8,128)(2,1)} fusion(f32[2048,768]{1,0:T(8,128)} %fusion.94, bf16[1024,2048]{1,0:T(8,128)(2,1)S(1)} %bitcast.221, bf16[1024,768]{1,0:T(8,128)(2,1)S(1)} %copy-done.60), kind=kOutput, calls=%fused_computation.60 | convolution fusion | flops 3224371200 | bytes 15204352 | tf_op jit(solution)/shard_map/dot_general | solution.py:38
  360.7 5.5 %fusion.33 = bf16[1,1,768,2048]{3,2,1,0:T(8,128)(2,1)} fusion(f32[768,2048]{1,0:T(8,128)S(1)} %fusion.48, bf16[1,1,1024,2048]{3,2,1,0:T(8,128)(2,1)S(1)} %copy-done.44, f32[1024]{0:T(1024)S(1)} %mul.178, f32[1024,768]{1,0:T(8,128)S(1)} %copy-done.56, f32[1024,768]{1,0:T(8,128)S(1)} %copy-done.55), kind=kOutput, calls=%fused_computation.61 | convolution fusion | flops 3232235520 | bytes 19927040 | tf_op jit(solution)/shard_map/dot_general | solution.py:38
  367.8 96.9 %reduce-scatter.5.cloned.1.call-done = bf16[1,64,2048]{2,1,0:T(8,128)(2,1)} async-done(((bf16[16,64,2048]{2,1,0:T(8,128)(2,1)}), bf16[1,64,2048]{2,1,0:T(8,128)(2,1)}) %reduce-scatter.5.cloned.1.call-update) | async-done | bytes 262160 | tf_op jit(solution)/shard_map/reduce_scatter | solution.py:158
  465.8 4.4 all-to-all-start.2
  (224 shorter events, 98.6 us)
Async XLA Ops:
  7.2 224.9 %all-gather.9.cloned.1.call-start = ((), (), s32[]{:S(2)}) async-start(), calls=%async_computation.8 | async-start | bytes 4456448 | tf_op jit(solution)/shard_map/all_gather | solution.py:73
  9.1 269.8 %all-gather.11.cloned.1.call-start = ((), (), s32[]{:S(2)}) async-start(), calls=%async_computation.9 | async-start | bytes 4456448 | tf_op jit(solution)/shard_map/all_gather | solution.py:73
  9.9 12.4 %copy-start.45 = (s32[1,4]{1,0:T(1,128)S(1)}, s32[1,4]{1,0:T(1,128)}, u32[]{:S(2)}) copy-start(s32[1,4]{1,0:T(1,128)} %param.11) | copy-start | bytes 52
  9.9 13.7 %copy-start.15 = (bf16[1,1,768,2048]{3,2,1,0:T(8,128)(2,1)S(1)}, bf16[1,1,768,2048]{3,2,1,0:T(8,128)(2,1)}, u32[]{:S(2)}) copy-start(bf16[1,1,768,2048]{3,2,1,0:T(8,128)(2,1)} %param.13) | copy-start | bytes 9437188
  17.1 182.9 %all-to-all-start = ((bf16[4,320,192]{1,2,0:T(8,128)(2,1)}), bf16[4,320,192]{1,2,0:T(8,128)(2,1)}, u32[]{:S(2)}, u32[]{:S(2)}) async-start(bf16[4,320,192]{1,2,0:T(8,128)(2,1)} %copy.142), calls=%async_computation | async-start | bytes 1179648 | tf_op jit(solution)/shard_map/all_to_all | solution.py:96
  22.2 276.8 %all-gather.7.cloned.1.call-start = ((), (), s32[]{:S(2)}) async-start(), calls=%async_computation.7 | async-start | bytes 6553600 | tf_op jit(solution)/shard_map/all_gather | solution.py:93
  26.7 177.6 %collective-permute-start = (bf16[2,192,2048]{2,1,0:T(8,128)(2,1)}, bf16[2,192,2048]{2,1,0:T(8,128)(2,1)}, u32[]{:S(2)}, u32[]{:S(2)}) collective-permute-start(bf16[2,192,2048]{2,1,0:T(8,128)(2,1)} %dynamic-slice_bitcast_fusion.1), channel_id=1, source_target_pairs={{0,2},{1,3},{2,0},{3,1},{4,6},{5,7},{6,4},{7,5},{8,10},{9,11},{10,... | collective-permute-start | bytes 4718600 | tf_op jit(solution)/shard_map/ppermute | solution.py:16
  35.2 166.9 %collective-permute-start.2 = (bf16[2,192,2048]{2,1,0:T(8,128)(2,1)}, bf16[2,192,2048]{2,1,0:T(8,128)(2,1)}, u32[]{:S(2)}, u32[]{:S(2)}) collective-permute-start(bf16[2,192,2048]{2,1,0:T(8,128)(2,1)} %dynamic-slice_bitcast_fusion), channel_id=1, source_target_pairs={{0,1},{1,0},{2,3},{3,2},{4,5},{5,4},{6,7},{7,6},{8,9},{9,8},{10,11... | collective-permute-start | bytes 4718600 | tf_op jit(solution)/shard_map/ppermute | solution.py:16
  40.3 327.5 %reduce-scatter.3.cloned.1.call-start = ((), (), s32[]{:S(2)}) async-start(), calls=%async_computation.5 | async-start | bytes 4456448 | tf_op jit(solution)/shard_map/reduce_scatter | solution.py:158
  40.3 7.5 %copy-start.39 = (s32[1,2,64,8]{2,3,1,0:T(8,128)S(1)}, s32[1,2,64,8]{2,3,1,0:T(8,128)}, u32[]{:S(2)}) copy-start(s32[1,2,64,8]{2,3,1,0:T(8,128)} %param.10) | copy-start | bytes 12292
  40.4 7.5 %copy-start.40 = (f32[1,2,64,8]{2,3,1,0:T(8,128)S(1)}, f32[1,2,64,8]{2,3,1,0:T(8,128)}, u32[]{:S(2)}) copy-start(f32[1,2,64,8]{2,3,1,0:T(8,128)} %param.9) | copy-start | bytes 12292
  169.7 6.8 %copy-start.18 = (bf16[1,1,2048,768]{3,2,1,0:T(8,128)(2,1)S(1)}, bf16[1,1,2048,768]{3,2,1,0:T(8,128)(2,1)}, u32[]{:S(2)}) copy-start(bf16[1,1,2048,768]{3,2,1,0:T(8,128)(2,1)} %param.12) | copy-start | bytes 9437188
  181.7 7.5 %copy-start.14 = (bf16[1,2,1,16,50,768]{5,3,4,2,1,0:T(8,128)(2,1)S(1)}, bf16[1,2,1,16,50,768]{5,3,4,2,1,0:T(8,128)(2,1)}, u32[]{:S(2)}) copy-start(bf16[1,2,1,16,50,768]{5,3,4,2,1,0:T(8,128)(2,1)} %param.15) | copy-start | bytes 7372804
  191.8 10.4 %copy-start.4 = (bf16[2048,768]{0,1:T(8,128)(2,1)S(1)}, bf16[2048,768]{0,1:T(8,128)(2,1)}, u32[]{:S(2)}) copy-start(bf16[2048,768]{0,1:T(8,128)(2,1)} %copy-done.3) | copy-start | bytes 9437188
  204.2 25.6 %collective-permute-start.3 = (bf16[192,2048]{1,0:T(8,128)(2,1)S(1)}, bf16[192,2048]{1,0:T(8,128)(2,1)S(1)}, u32[]{:S(2)}, u32[]{:S(2)}) collective-permute-start(bf16[192,2048]{1,0:T(8,128)(2,1)S(1)} %dynamic-slice_bitcast_fusion.2), channel_id=1, source_target_pairs={{0,2},{1,3},{2,0},{3,1},{4,6},{5,7},{6,4},{7,5},{8,10},{9,11},{10,... | collective-permute-start | bytes 2359304 | tf_op jit(solution)/shard_map/ppermute | solution.py:16
  206.9 25.3 %copy-start.12 = (bf16[2,192,2048]{2,1,0:T(8,128)(2,1)}, bf16[2,192,2048]{2,1,0:T(8,128)(2,1)S(1)}, u32[]{:S(2)}) copy-start(bf16[2,192,2048]{2,1,0:T(8,128)(2,1)S(1)} %bitcast_add_fusion.1) | copy-start | bytes 4718596
  206.9 25.2 %collective-permute-start.1 = (bf16[192,2048]{1,0:T(8,128)(2,1)S(1)}, bf16[192,2048]{1,0:T(8,128)(2,1)}, u32[]{:S(2)}, u32[]{:S(2)}) collective-permute-start(bf16[192,2048]{1,0:T(8,128)(2,1)S(1)} %dynamic-slice_bitcast_fusion.3), channel_id=1, source_target_pairs={{0,1},{1,0},{2,3},{3,2},{4,5},{5,4},{6,7},{7,6},{8,9},{9,8},{10,11... | collective-permute-start | bytes 2359304 | tf_op jit(solution)/shard_map/ppermute | solution.py:16
  229.9 19.5 %copy-start.5 = (bf16[192,2048]{1,0:T(8,128)(2,1)}, bf16[192,2048]{1,0:T(8,128)(2,1)S(1)}, u32[]{:S(2)}) copy-start(bf16[192,2048]{1,0:T(8,128)(2,1)S(1)} %bitcast_add_fusion.2) | copy-start | bytes 2359300
  232.1 7.4 %copy-start.49 = (f32[1024,768]{1,0:T(8,128)S(1)}, f32[1024,768]{1,0:T(8,128)}, u32[]{:S(2)}) copy-start(f32[1024,768]{1,0:T(8,128)} %fusion.22) | copy-start | bytes 9437188
  239.5 9.9 %copy-start.31 = (bf16[1024,192]{0,1:T(8,128)(2,1)}, bf16[1024,192]{0,1:T(8,128)(2,1)S(1)}, u32[]{:S(2)}) copy-start(bf16[1024,192]{0,1:T(8,128)(2,1)S(1)} %get-tuple-element.87) | copy-start | bytes 1179652
  252.7 211.9 %reduce-scatter.5.cloned.1.call-start = ((), (), s32[]{:S(2)}) async-start(), calls=%async_computation.6 | async-start | bytes 4456448 | tf_op jit(solution)/shard_map/reduce_scatter | solution.py:158
  254.7 12.8 %copy-start = (bf16[1,1,1,16,50,2048]{5,3,4,2,1,0:T(8,128)(2,1)S(1)}, bf16[1,1,1,16,50,2048]{5,3,4,2,1,0:T(8,128)(2,1)}, u32[]{:S(2)}) copy-start(bf16[1,1,1,16,50,2048]{5,3,4,2,1,0:T(8,128)(2,1)} %get-tuple-element.62) | copy-start | bytes 9830404
  272.3 6.6 %copy-start.13 = (bf16[2,192,2048]{2,1,0:T(8,128)(2,1)S(1)}, bf16[2,192,2048]{2,1,0:T(8,128)(2,1)}, u32[]{:S(2)}) copy-start(bf16[2,192,2048]{2,1,0:T(8,128)(2,1)} %copy-done.12) | copy-start | bytes 4718596
  278.9 6.7 %copy-start.54 = (f32[1024,768]{1,0:T(8,128)S(1)}, f32[1024,768]{1,0:T(8,128)}, u32[]{:S(2)}) copy-start(f32[1024,768]{1,0:T(8,128)} %fusion.20) | copy-start | bytes 9437188
  285.6 6.6 %copy-start.21 = (bf16[1,1,2048,768]{3,2,1,0:T(8,128)(2,1)S(1)}, bf16[1,1,2048,768]{3,2,1,0:T(8,128)(2,1)}, u32[]{:S(2)}) copy-start(bf16[1,1,2048,768]{3,2,1,0:T(8,128)(2,1)} %param.12) | copy-start | bytes 9437188
  311.4 7.1 %copy-start.7 = (bf16[1024,2048]{1,0:T(8,128)(2,1)}, bf16[1024,2048]{1,0:T(8,128)(2,1)S(1)}, u32[]{:S(2)}) copy-start(bf16[1024,2048]{1,0:T(8,128)(2,1)S(1)} %convolution_convert_fusion.1) | copy-start | bytes 12582916
  330.8 135.0 %all-to-all-start.1 = ((bf16[4,320,192]{1,2,0:T(8,128)(2,1)}), bf16[4,320,192]{1,2,0:T(8,128)(2,1)S(1)}, u32[]{:S(2)}, u32[]{:S(2)}) async-start(bf16[4,320,192]{1,2,0:T(8,128)(2,1)} %copy.151), calls=%async_computation.3 | async-start | bytes 1179648 | tf_op jit(solution)/shard_map/all_to_all | solution.py:184
  353.6 7.1 %copy-start.55 = (f32[1024,768]{1,0:T(8,128)S(1)}, f32[1024,768]{1,0:T(8,128)}, u32[]{:S(2)}) copy-start(f32[1024,768]{1,0:T(8,128)} %fusion.20) | copy-start | bytes 9437188
  353.6 7.1 %copy-start.56 = (f32[1024,768]{1,0:T(8,128)S(1)}, f32[1024,768]{1,0:T(8,128)}, u32[]{:S(2)}) copy-start(f32[1024,768]{1,0:T(8,128)} %get-tuple-element.73) | copy-start | bytes 9437188
  360.6 104.0 %copy-start.28 = (bf16[1,2,64,2048]{3,2,1,0:T(8,128)(2,1)S(1)}, bf16[1,2,64,2048]{3,2,1,0:T(8,128)(2,1)}, u32[]{:S(2)}) copy-start(bf16[1,2,64,2048]{3,2,1,0:T(8,128)(2,1)} %param.8) | copy-start | bytes 1572868
  465.8 14.7 %all-to-all-start.2 = ((bf16[192,4,512]{2,0,1:T(8,128)(2,1)}), bf16[192,4,512]{2,0,1:T(8,128)(2,1)}, u32[]{:S(2)}, u32[]{:S(2)}) async-start(bf16[192,4,512]{2,0,1:T(8,128)(2,1)} %bitcast.207), calls=%async_computation.4 | async-start | bytes 1572864 | tf_op jit(solution)/shard_map/all_to_all | solution.py:180
  471.1 11.8 %collective-permute-start.4 = (bf16[2,64,2048]{2,1,0:T(8,128)(2,1)}, bf16[2,64,2048]{2,1,0:T(8,128)(2,1)}, u32[]{:S(2)}, u32[]{:S(2)}) collective-permute-start(bf16[2,64,2048]{2,1,0:T(8,128)(2,1)} %pad_maximum_fusion.1), channel_id=1, source_target_pairs={{16,0},{0,16},{17,1},{1,17},{18,2},{2,18},{19,3},{3,19},{20,4},{4,... | collective-permute-start | bytes 1572872 | tf_op jit(solution)/shard_map/ppermute | solution.py:22
  (42 other events, 169.3 us)
Sparse Core Ops, SparseCore 0:
  11.3 106.0 all-gather.8
  120.2 74.9 all-gather.10
  197.0 67.0 all-gather.6
  266.3 101.4 reduce-scatter.2
  369.9 94.6 reduce-scatter.4

commit v2 on v1

--- a/solution.py
+++ b/solution.py
@@ -24,6 +24,29 @@
 
 def pick(array, index, axis):
     return lax.dynamic_index_in_dim(array, index, axis, keepdims=False)
+
+
+def offsets(bits):
+    found = [0]
+    for bit in bits:
+        found = found + [value ^ 2**bit for value in found]
+    return found
+
+
+def spread(block, bits):
+    for bit in bits:
+        block = jnp.concatenate([block, partner(block, "expert", bit)], 0)
+    return block
+
+
+def collect(total, bits):
+    for bit in reversed(bits):
+        half = total.shape[0] // 2
+        kept, sent = total[:half], total[half:].astype(BF16)
+        total = kept.astype(F32) + partner(sent, "expert", bit).astype(F32)
+        if half > 1:
+            total = total.astype(BF16)
+    return total
 
 
 def dot_nn(a, b):
@@ -68,9 +91,12 @@
     is_owner = local_pos == owner_pos
     hot_expert = REPL * group_id + owner_pos
 
+    bits = experts.bit_length() - 1
+    orders = [list(range(2, bits)) + pair for pair in ([1, 0], [0, 1])]
+    group_orders = [[0, 1], [1, 0]]
     meta = jnp.concatenate([expert_ids[0].astype(F32), route_weights[0]], -1)
-    meta = lax.all_gather(meta, "expert", axis=1)
-    grads = [lax.all_gather(grad_out[0, b], "expert", axis=0, tiled=True) for b in range(MB)]
+    meta = spread(meta.transpose(0, 2, 1)[None], orders[0])
+    grads = [spread(grad_out[0, b][None], orders[b % 2]) for b in range(MB)]
 
     own_up = up_weight[0, 0]
     own_down = down_weight[0, 0]
@@ -89,58 +115,63 @@
     inputs = saved_inputs[0, :, 0]
     gates = saved_gates[0, :, 0]
     hot_rows = experts * quarter_rows
-    hot_inputs = inputs[:, :, most:].reshape(MB * hot_rows, features)
-    hot_inputs = lax.all_gather(hot_inputs, "expert", axis=0, axis_index_groups=groups)
-    hot_inputs = hot_inputs.reshape(REPL, MB, hot_rows, features)
+    hot_inputs = inputs[:, :, most:].reshape(MB, hot_rows, features)
+    hot_inputs = [
+        spread(hot_inputs[b][None], group_orders[b % 2]).reshape(REPL * hot_rows, features)
+        for b in range(MB)
+    ]
     hot_gates = gates[:, :, most:].reshape(MB * hot_rows, REPL, quarter).transpose(1, 0, 2)
     hot_gates = lax.all_to_all(hot_gates, "expert", 0, 0, axis_index_groups=groups, tiled=True)
     hot_gates = hot_gates.reshape(REPL, MB, hot_rows, quarter)
 
-    ids = meta[..., :TOP]
-    weights = meta[..., TOP:]
-    own_hit = (ids == device.astype(F32)) & jnp.logical_not(is_owner)
-    hot_hit = ids == hot_expert.astype(F32)
-    own_weight = jnp.sum(jnp.where(own_hit, weights, 0.0), -1)
-    hot_weight = jnp.sum(jnp.where(hot_hit, weights, 0.0), -1)
-    own_named = jnp.any(own_hit, -1)
-    hot_named = jnp.any(hot_hit, -1)
-    own_place = jnp.where(own_named, jnp.cumsum(own_named.astype(jnp.int32), -1) - 1, -1)
-    hot_place = jnp.where(hot_named, jnp.cumsum(hot_named.astype(jnp.int32), -1) - 1, -1)
-    own_select = (own_place[..., None] == jnp.arange(slots, dtype=jnp.int32)).astype(BF16)
-    block = jnp.arange(experts, dtype=jnp.int32)
-    replica = jnp.arange(REPL, dtype=jnp.int32)
-    order = (
-        REPL * jnp.arange(quarter_rows, dtype=jnp.int32)[None, None, :]
-        + (replica[:, None, None] - block[None, :, None]) % REPL
-    )
-    same = block[:, None, None, None, None] == block[None, None, None, :, None]
-    hot_select = [
-        ((hot_place[b][:, :, None, None, None] == order[None, None]) & same)
-        .astype(BF16)
-        .reshape(experts * tokens, REPL * hot_rows)
-        for b in range(MB)
-    ]
-
+    own_select, hot_select, hot_gate_select, own_weight, hot_weight = [], [], [], [], []
+    earlier = jnp.triu(jnp.ones((tokens, tokens), BF16), 1)
+    for b in range(MB):
+        order = offsets(orders[b % 2])
+        first = offsets(orders[0])
+        table = meta[:, b]
+        if order != first:
+            table = jnp.stack([table[first.index(value)] for value in order], 0)
+        table = table.transpose(1, 0, 2)
+        block = (jnp.array(order, jnp.int32) ^ device)[:, None]
+        own_hit = (table[:TOP] == device.astype(F32)) & jnp.logical_not(is_owner)
+        hot_hit = table[:TOP] == hot_expert.astype(F32)
+        own_weight.append(jnp.sum(jnp.where(own_hit, table[TOP:], 0.0), 0).reshape(-1, 1))
+        hot_weight.append(jnp.sum(jnp.where(hot_hit, table[TOP:], 0.0), 0).reshape(-1, 1))
+        own_named = jnp.sum(own_hit.astype(F32), 0)
+        hot_named = jnp.sum(hot_hit.astype(F32), 0)
+        own_rank = dot_nn(own_named.astype(BF16), earlier).astype(jnp.int32)
+        hot_rank = dot_nn(hot_named.astype(BF16), earlier).astype(jnp.int32)
+        own_slot = jnp.where(own_named > 0, block * slots + own_rank, -1)
+        target = (block + hot_rank) % REPL
+        row = block * quarter_rows + hot_rank // REPL
+        away = target ^ local_pos
+        if group_orders[b % 2] == [1, 0]:
+            away = away // 2 + 2 * (away % 2)
+        near_slot = jnp.where(hot_named > 0, away * hot_rows + row, -1)
+        far_slot = jnp.where(hot_named > 0, target * hot_rows + row, -1)
+        slot_range = jnp.arange(experts * slots, dtype=jnp.int32)[None]
+        hot_range = jnp.arange(REPL * hot_rows, dtype=jnp.int32)[None]
+        own_select.append((own_slot.reshape(-1, 1) == slot_range).astype(BF16))
+        hot_select.append((near_slot.reshape(-1, 1) == hot_range).astype(BF16))
+        hot_gate_select.append((far_slot.reshape(-1, 1) == hot_range).astype(BF16))
+
+    flat_inputs = inputs.reshape(MB, experts * slots, features)
+    flat_gates = gates.reshape(MB, experts * slots, hidden_units)
     parts = []
     returned = []
     gate_grads = []
     hot_gate_grads = []
     for b in range(MB):
-        own_x = jnp.einsum(
-            "etc,ecd->etd", own_select[b], inputs[b], preferred_element_type=F32
-        ).astype(BF16).reshape(experts * tokens, features)
-        own_a = jnp.einsum(
-            "etc,ecd->etd", own_select[b], gates[b], preferred_element_type=F32
-        ).astype(BF16).reshape(experts * tokens, hidden_units)
-        hot_x = dot_nn(
-            hot_select[b], hot_inputs[:, b].reshape(REPL * hot_rows, features)
+        own_x = dot_nn(own_select[b], flat_inputs[b]).astype(BF16)
+        own_a = dot_nn(own_select[b], flat_gates[b]).astype(BF16)
+        hot_x = dot_nn(hot_select[b], hot_inputs[b]).astype(BF16)
+        hot_a = dot_nn(
+            hot_gate_select[b], hot_gates[:, b].reshape(REPL * hot_rows, quarter)
         ).astype(BF16)
-        hot_a = dot_nn(
-            hot_select[b], hot_gates[:, b].reshape(REPL * hot_rows, quarter)
-        ).astype(BF16)
-        grad = grads[b].astype(F32)
-        own_g = (own_weight[b].reshape(-1, 1) * grad).astype(BF16)
-        hot_g = (hot_weight[b].reshape(-1, 1) * grad).astype(BF16)
+        grad = grads[b].reshape(experts * tokens, features).astype(F32)
+        own_g = (own_weight[b] * grad).astype(BF16)
+        hot_g = (hot_weight[b] * grad).astype(BF16)
         own_act, own_slope = gate_parts(own_a)
         hot_act, hot_slope = gate_parts(hot_a)
         own_uv = dot_nn(own_x, own_up)
@@ -155,18 +186,13 @@
         hot_gg = (hot_gh * hot_uv * hot_slope).astype(BF16)
         term = (dot_nt(own_gu, own_up) + dot_nn(hot_gu, hot_up)).astype(BF16)
         returned.append(
-            lax.psum_scatter(term.reshape(experts, tokens, features), "expert")
+            collect(term.reshape(experts, tokens, features), orders[b % 2])[0]
         )
         gate_grads.append(
-            jnp.einsum(
-                "etc,etf->ecf",
-                own_select[b],
-                own_gg.reshape(experts, tokens, hidden_units),
-                preferred_element_type=F32,
-            ).astype(BF16)
+            dot_tn(own_select[b], own_gg).astype(BF16).reshape(experts, slots, hidden_units)
         )
         hot_gate_grads.append(
-            dot_tn(hot_select[b], hot_gg).astype(BF16).reshape(REPL, hot_rows, quarter)
+            dot_tn(hot_gate_select[b], hot_gg).astype(BF16).reshape(REPL, hot_rows, quarter)
         )
         parts.append((own_x, own_gu, own_hidden, own_g, hot_x, hot_gu, hot_hidden, hot_g))
     own_x, own_gu, own_hidden, own_g, hot_x, hot_gu, hot_hidden, hot_g = (
@@ -185,14 +211,15 @@
     back = back.transpose(1, 0, 2).reshape(MB, experts, quarter_rows, hidden_units)
     gate_grad = jnp.concatenate([jnp.stack(gate_grads, 0)[:, :, :most], back], 2)
 
-    token_grads = jnp.stack(
+    sent_back = jnp.stack(
         [
-            (returned[b].astype(F32) + grad_out[0, b].astype(F32)).astype(BF16)
+            from_behind(
+                (returned[b] + grad_out[0, b].astype(F32)).astype(BF16), "pipe", -1
+            )
             for b in range(MB)
         ],
         0,
     )
-    sent_back = from_behind(token_grads, "pipe", -1)
     return (
         sent_back[None],
         up_grad[None, None],

time: 497 us -> 481 us (0.968)
  blocking collectives: 84.4 us -> 0 us
  starting transfers between devices: 17.5 us -> 49.8 us
  waiting for transfers between devices: 123 us -> 144 us
  local copies, waits for them, and re-layouts: 78.8 us -> 97.7 us
  between operations: 16.2 us -> 2.95 us
  matrix products: 120 us -> 127 us
    ppermute x4 -> x28, waiting for transfers between devices: 22.4 us -> 143 us  [partner(): return lax.ppermute(value, axis, pairs)]
    reduce_scatter x2 -> x0, waiting for transfers between devices: 98.6 us -> none  [per_device(): lax.psum_scatter(term.reshape(experts, tokens, features), 'expert')]
    all_gather x1 -> x0, blocking collectives: 84.4 us -> none  [per_device(): meta = lax.all_gather(meta, 'expert', axis=1)]
    reduce_or x1 -> x0, other arithmetic: 35.8 us -> none  [per_device(): own_named = jnp.any(own_hit, -1)]
    ppermute x4 -> x28, starting transfers between devices: 4.11 us -> 36.1 us  [partner(): return lax.ppermute(value, axis, pairs)]
    convert_element_type x3 -> x11, other arithmetic: 1.16 us -> 25 us  [the longest x4 18 us: per_device(): own_g = (own_weight[b] * grad).astype(BF16)]
    dot_general x6 -> x0, matrix products: 22 us -> none  [the longest x2 11.6 us: per_device(): jnp.einsum('etc,ecd->etd', own_select[b], inputs[b], preferred_element_ty...]
    dot_general x8 -> x16, matrix products: 29.1 us -> 47.3 us  [dot_nn(): return jnp.dot(a, b, preferred_element_type=F32)]
  transfers between devices with their start and end apart: 13 -> 33, of which waited for: 5 -> 15; matrix products, arithmetic and copies ran while one was open for 48% -> 52% of each run, Pallas kernels for 0% -> 0%
where the time goes in v2:
time: 481 us; the launch traced here: 476 us
  waiting for transfers between devices  144 us (30%)
  matrix products  127 us (26%)
  local copies, waits for them, and re-layouts  97.7 us (20%)
  other arithmetic  55 us (11%)
  starting transfers between devices  49.8 us (10%)
    ppermute x28, waiting for transfers between devices, partner(): return lax.ppermute(value, axis, pairs)  143 us
    dot_general x12, matrix products, dot_tn(): lax.dot_general(a, b, (((0,), (0,)), ((), ())), preferred_element_type=F32)  49 us
    dot_general x16, matrix products, dot_nn(): return jnp.dot(a, b, preferred_element_type=F32)  47.3 us
    ppermute x28, starting transfers between devices, partner(): return lax.ppermute(value, axis, pairs)  36.1 us
    unnamed x130, local copies, waits for them, and re-layouts  30.9 us
    dot_general x8, matrix products, dot_nt(): lax.dot_general(a, b, (((1,), (1,)), ((), ())), preferred_element_type=F32)  30.7 us
    convert_element_type x4, other arithmetic, per_device(): own_g = (own_weight[b] * grad).astype(BF16)  18 us
    slice x3, local copies, waits for them, and re-layouts, per_device(): own_x = dot_nn(own_select[b], flat_inputs[b]).astype(BF16)  14.9 us
  transfers between devices with their start and end apart: 33, of which 15 were waited for; matrix products, arithmetic and copies ran while one was open for 52% of the time, Pallas kernels for 0%

profile of v2, /device:TPU:0, one launch (start us, length us, event | category | flops | bytes accessed | tf_op | source)
XLA Modules:
  0.0 476.1 jit_solution(17065084568496599252)
XLA Ops:
  25.5 4.3 all-to-all-start
  34.1 5.6 %fusion.151 = (bf16[1,1,1,16,50,2048]{5,3,4,2,1,0:T(8,128)(2,1)}, bf16[1,1,1,16,50,2048]{5,3,4,2,1,0:T(8,128)(2,1)S(1)}) fusion(bf16[1,2,1,16,50,2048]{5,3,4,2,1,0:T(8,128)(2,1)} %param.16), kind=kLoop, calls=%fused_computation.317 | loop fusion | bytes 13107200 | tf_op jit(solution)/shard_map/slice | solution.py:166
  51.0 5.6 %copy.82 = bf16[1,1,1,16,50,2048]{5,4,3,2,1,0:T(8,128)(2,1)} copy(bf16[1,1,1,16,50,2048]{5,3,4,2,1,0:T(8,128)(2,1)} %get-tuple-element.38) | data formatting | bytes 6553600 | tf_op jit(solution)/shard_map/slice | solution.py:166
  56.6 4.7 squeeze.89
  70.1 4.8 %squeeze.88 = bf16[800,2048]{1,0:T(8,128)(2,1)} reshape(bf16[1,1,1,16,50,2048]{5,4,3,2,1,0:T(8,128)(2,1)} %copy.81) | data formatting | bytes 6553600 | tf_op jit(solution)/shard_map/squeeze | solution.py:166
  87.7 4.3 collective-permute-done.3
  108.6 7.2 %convolution_convert_fusion.2 = bf16[1024,2048]{1,0:T(8,128)(2,1)S(1)} fusion(bf16[800,2048]{1,0:T(8,128)(2,1)} %squeeze.89, s32[1024]{0:T(1024)S(1)} %eq.142), kind=kOutput, calls=%fused_computation.31 | convolution fusion | flops 3358359552 | bytes 7475200 | tf_op jit(solution)/shard_map/dot_general | solution.py:53
  115.9 5.2 %fusion.28 = f32[1024,768]{1,0:T(8,128)} fusion(bf16[1024,2048]{1,0:T(8,128)(2,1)S(1)} %convolution_convert_fusion.2, bf16[1,1,2048,768]{3,2,1,0:T(8,128)(2,1)S(1)} %copy-done.16), kind=kOutput, calls=%fused_computation.53 | convolution fusion | flops 3221225472 | bytes 10485760 | tf_op jit(solution)/shard_map/dot_general | solution.py:53
  124.3 7.4 %convolution_convert_fusion.3 = bf16[1024,2048]{1,0:T(8,128)(2,1)S(1)} fusion(bf16[800,2048]{1,0:T(8,128)(2,1)} %squeeze.88, s32[1024]{0:T(1024)S(1)} %eq.131), kind=kOutput, calls=%fused_computation.32 | convolution fusion | flops 3358359552 | bytes 7475200 | tf_op jit(solution)/shard_map/dot_general | solution.py:53
  131.7 5.1 %fusion.30 = f32[1024,768]{1,0:T(8,128)} fusion(bf16[1024,2048]{1,0:T(8,128)(2,1)S(1)} %convolution_convert_fusion.3, bf16[1,1,2048,768]{3,2,1,0:T(8,128)(2,1)S(1)} %copy-done.17), kind=kOutput, calls=%fused_computation.55 | convolution fusion | flops 3221225472 | bytes 10485760 | tf_op jit(solution)/shard_map/dot_general | solution.py:53
  155.2 20.6 %collective-permute-done.18 = bf16[2,64,2048]{2,1,0:T(8,128)(2,1)S(1)} collective-permute-done((bf16[2,64,2048]{2,1,0:T(8,128)(2,1)S(1)}, bf16[2,64,2048]{2,1,0:T(8,128)(2,1)S(1)}, u32[]{:S(2)}, u32[]{:S(2)}) %collective-permute-start.18) | collective-permute-done | bytes 524320 | tf_op jit(solution)/shard_map/ppermute | solution.py:16
  178.2 7.4 %collective-permute-done.5 = bf16[2,64,2048]{2,1,0:T(8,128)(2,1)S(1)} collective-permute-done((bf16[2,64,2048]{2,1,0:T(8,128)(2,1)S(1)}, bf16[2,64,2048]{2,1,0:T(8,128)(2,1)S(1)}, u32[]{:S(2)}, u32[]{:S(2)}) %collective-permute-start.5) | collective-permute-done | bytes 524320 | tf_op jit(solution)/shard_map/ppermute | solution.py:16
  193.6 15.9 %collective-permute-done.19 = bf16[4,64,2048]{2,1,0:T(8,128)(2,1)S(1)} collective-permute-done((bf16[4,64,2048]{2,1,0:T(8,128)(2,1)S(1)}, bf16[4,64,2048]{2,1,0:T(8,128)(2,1)S(1)}, u32[]{:S(2)}, u32[]{:S(2)}) %collective-permute-start.19) | collective-permute-done | bytes 1048608 | tf_op jit(solution)/shard_map/ppermute | solution.py:16
  212.3 17.6 %collective-permute-done.6 = bf16[4,64,2048]{2,1,0:T(8,128)(2,1)S(1)} collective-permute-done((bf16[4,64,2048]{2,1,0:T(8,128)(2,1)S(1)}, bf16[4,64,2048]{2,1,0:T(8,128)(2,1)S(1)}, u32[]{:S(2)}, u32[]{:S(2)}) %collective-permute-start.6) | collective-permute-done | bytes 1048608 | tf_op jit(solution)/shard_map/ppermute | solution.py:16
  250.9 21.2 %collective-permute-done.7 = bf16[8,64,2048]{2,1,0:T(8,128)(2,1)S(1)} collective-permute-done((bf16[8,64,2048]{2,1,0:T(8,128)(2,1)S(1)}, bf16[8,64,2048]{2,1,0:T(8,128)(2,1)S(1)}, u32[]{:S(2)}, u32[]{:S(2)}) %collective-permute-start.7) | collective-permute-done | bytes 2097184 | tf_op jit(solution)/shard_map/ppermute | solution.py:16
  280.3 5.6 %fusion.5 = (bf16[1024,2048]{1,0:T(8,128)(2,1)}, bf16[1024,2048]{1,0:T(8,128)(2,1)S(1)}) fusion(bf16[16,64,2048]{2,1,0:T(8,128)(2,1)} %constant_dynamic-update-slice_fusion.5, f32[1024]{0:T(1024)S(1)} %mul.232, f32[1024]{0:T(1024)S(1)} %mul.206), kind=kLoop, calls=%fused_computation.11 | loop fusion | flops 10485760 | bytes 12591104 | tf_op jit(solution)/shard_map/convert_element_type | solution.py:173
  291.6 5.9 %fusion.34 = f32[1024,2048]{1,0:T(8,128)} fusion(bf16[1,1,2048,768]{3,2,1,0:T(8,128)(2,1)S(1)} %copy-done.18, f32[1024,768]{1,0:T(8,128)S(1)} %fusion.38, bf16[1024,768]{1,0:T(8,128)(2,1)S(1)} %copy-done.47), kind=kOutput, calls=%fused_computation.59 | convolution fusion | flops 3226730496 | bytes 16252928 | tf_op jit(solution)/shard_map/dot_general | solution.py:57
  297.5 6.1 %fusion.149 = f32[2048,768]{1,0:T(8,128)} fusion(bf16[1024,2048]{1,0:T(8,128)(2,1)S(1)} %copy-done.42, f32[1024,768]{1,0:T(8,128)S(1)} %fusion.38, bf16[1024,768]{1,0:T(8,128)(2,1)S(1)} %copy-done.47), kind=kOutput, calls=%fused_computation.315 | convolution fusion | flops 3226730496 | bytes 15204352 | tf_op jit(solution)/shard_map/dot_general | solution.py:61
  305.2 4.9 %fusion = bf16[16,64,2048]{2,1,0:T(8,128)(2,1)} fusion(bf16[16,64,2048]{2,1,0:T(8,128)(2,1)} %constant_dynamic-update-slice_fusion.26, f32[16,64]{1,0:T(8,128)S(1)} %get-tuple-element.27), kind=kLoop, calls=%fused_computation.3 | loop fusion | flops 6291456 | bytes 8392704 | tf_op jit(solution)/shard_map/convert_element_type | solution.py:173
  310.1 4.5 fusion.2
  325.9 4.6 all-to-all-start.1
  330.6 6.4 %fusion.36 = f32[1024,768]{1,0:T(8,128)S(1)} fusion(bf16[1024,2048]{1,0:T(8,128)(2,1)} %bitcast.248, bf16[1,1,768,2048]{3,2,1,0:T(8,128)(2,1)} %param.15), kind=kOutput, calls=%fused_computation.62 | convolution fusion | flops 3221225472 | bytes 10485760 | tf_op jit(solution)/shard_map/dot_general | solution.py:57
  349.0 5.7 %fusion.60 = f32[768,2048]{1,0:T(8,128)} fusion(bf16[1024,2048]{1,0:T(8,128)(2,1)S(1)} %copy-done.12, f32[1024,768]{1,0:T(8,128)S(1)} %copy-done.36, bf16[1024,768]{1,0:T(8,128)(2,1)S(1)} %copy-done.37), kind=kOutput, calls=%fused_computation.102 | convolution fusion | flops 3226730496 | bytes 15204352 | tf_op jit(solution)/shard_map/dot_general | solution.py:61
  354.8 8.7 %fusion.41 = bf16[1,1,768,2048]{3,2,1,0:T(8,128)(2,1)} fusion(f32[768,2048]{1,0:T(8,128)} %fusion.60, bf16[1024,2048]{1,0:T(8,128)(2,1)S(1)} %copy-done.11, f32[1024,768]{1,0:T(8,128)} %fusion.30, bf16[1024,768]{1,0:T(8,128)(2,1)} %fusion.58), kind=kOutput, calls=%fused_computation.71 | convolution fusion | flops 3229876224 | bytes 18350080 | tf_op jit(solution)/shard_map/dot_general | solution.py:61
  363.5 4.6 fusion.66
  368.1 8.3 %fusion.40 = bf16[1,1,2048,768]{3,2,1,0:T(8,128)(2,1)} fusion(f32[2048,768]{1,0:T(8,128)} %fusion.149, bf16[1024,2048]{1,0:T(8,128)(2,1)S(1)} %copy-done.40, f32[1024,768]{1,0:T(8,128)} %copy-done.46, bf16[1024,768]{1,0:T(8,128)(2,1)S(1)} %copy-done.38), kind=kOutput, calls=%fused_computation.70 | convolution fusion | flops 3229876224 | bytes 18350080 | tf_op jit(solution)/shard_map/dot_general | solution.py:61
  376.4 7.4 %collective-permute-done.21 = bf16[8,64,2048]{2,1,0:T(8,128)(2,1)S(1)} collective-permute-done((bf16[8,64,2048]{2,1,0:T(8,128)(2,1)S(1)}, bf16[8,64,2048]{2,1,0:T(8,128)(2,1)S(1)}, u32[]{:S(2)}, u32[]{:S(2)}) %collective-permute-start.21) | collective-permute-done | bytes 2097184 | tf_op jit(solution)/shard_map/ppermute | solution.py:16
  399.7 8.6 %collective-permute-done.22 = bf16[4,64,2048]{2,1,0:T(8,128)(2,1)S(1)} collective-permute-done((bf16[4,64,2048]{2,1,0:T(8,128)(2,1)S(1)}, bf16[4,64,2048]{2,1,0:T(8,128)(2,1)S(1)}, u32[]{:S(2)}, u32[]{:S(2)}) %collective-permute-start.22) | collective-permute-done | bytes 1048608 | tf_op jit(solution)/shard_map/ppermute | solution.py:16
  418.2 20.6 %collective-permute-done.23 = bf16[2,64,2048]{2,1,0:T(8,128)(2,1)S(1)} collective-permute-done((bf16[2,64,2048]{2,1,0:T(8,128)(2,1)}, bf16[2,64,2048]{2,1,0:T(8,128)(2,1)S(1)}, u32[]{:S(2)}, u32[]{:S(2)}) %collective-permute-start.23) | collective-permute-done | bytes 524320 | tf_op jit(solution)/shard_map/ppermute | solution.py:16
  440.8 9.3 %collective-permute-done.14 = bf16[2,64,2048]{2,1,0:T(8,128)(2,1)} collective-permute-done((bf16[2,64,2048]{2,1,0:T(8,128)(2,1)}, bf16[2,64,2048]{2,1,0:T(8,128)(2,1)}, u32[]{:S(2)}, u32[]{:S(2)}) %collective-permute-start.14) | collective-permute-done | bytes 524320 | tf_op jit(solution)/shard_map/ppermute | solution.py:16
  452.9 4.2 fusion.51
  457.1 4.3 all-to-all-start.2
  (301 shorter events, 216.6 us)
Async XLA Ops:
  2.7 73.0 %collective-permute-start = (f32[1,2,16,64]{3,2,0,1:T(8,128)}, f32[1,2,16,64]{3,2,0,1:T(8,128)S(1)}, u32[]{:S(2)}, u32[]{:S(2)}) collective-permute-start(f32[1,2,16,64]{3,2,0,1:T(8,128)} %get-tuple-element.62), channel_id=1, source_target_pairs={{0,4},{1,5},{2,6},{3,7},{4,0},{5,1},{6,2},{7,3},{8,12},{9,13},{10,... | collective-permute-start | bytes 24584 | tf_op jit(solution)/shard_map/ppermute | solution.py:16
  7.5 132.3 %collective-permute-start.17 = (bf16[1,64,2048]{2,1,0:T(8,128)(2,1)}, bf16[1,64,2048]{2,1,0:T(8,128)(2,1)S(1)}, u32[]{:S(2)}, u32[]{:S(2)}) collective-permute-start(bf16[1,64,2048]{2,1,0:T(8,128)(2,1)} %get-tuple-element.55), channel_id=1, source_target_pairs={{0,4},{1,5},{2,6},{3,7},{4,0},{5,1},{6,2},{7,3},{8,12},{9,13},{10,... | collective-permute-start | bytes 786440 | tf_op jit(solution)/shard_map/ppermute | solution.py:16
  15.9 171.3 %collective-permute-start.10 = (bf16[2,192,2048]{2,1,0:T(8,128)(2,1)}, bf16[2,192,2048]{2,1,0:T(8,128)(2,1)}, u32[]{:S(2)}, u32[]{:S(2)}) collective-permute-start(bf16[2,192,2048]{2,1,0:T(8,128)(2,1)} %dynamic-slice_bitcast_fusion), channel_id=1, source_target_pairs={{0,1},{1,0},{2,3},{3,2},{4,5},{5,4},{6,7},{7,6},{8,9},{9,8},{10,11... | collective-permute-start | bytes 4718600 | tf_op jit(solution)/shard_map/ppermute | solution.py:16
  20.7 130.9 %collective-permute-start.28 = (bf16[1,160,2048]{2,1,0:T(8,128)(2,1)}, bf16[1,160,2048]{2,1,0:T(8,128)(2,1)}, u32[]{:S(2)}, u32[]{:S(2)}) collective-permute-start(bf16[1,160,2048]{2,1,0:T(8,128)(2,1)} %slice.323), channel_id=1, source_target_pairs={{0,2},{1,3},{2,0},{3,1},{4,6},{5,7},{6,4},{7,5},{8,10},{9,11},{10,... | collective-permute-start | bytes 1966088 | tf_op jit(solution)/shard_map/ppermute | solution.py:16
  25.5 121.3 %all-to-all-start = ((bf16[4,320,192]{1,2,0:T(8,128)(2,1)}), bf16[4,320,192]{1,2,0:T(8,128)(2,1)}, u32[]{:S(2)}, u32[]{:S(2)}) async-start(bf16[4,320,192]{1,2,0:T(8,128)(2,1)} %copy.78), calls=%async_computation | async-start | bytes 1179648 | tf_op jit(solution)/shard_map/all_to_all | solution.py:124
  31.3 121.8 %collective-permute-start.26 = (bf16[1,160,2048]{2,1,0:T(8,128)(2,1)}, bf16[1,160,2048]{2,1,0:T(8,128)(2,1)}, u32[]{:S(2)}, u32[]{:S(2)}) collective-permute-start(bf16[1,160,2048]{2,1,0:T(8,128)(2,1)} %slice.321), channel_id=1, source_target_pairs={{0,1},{1,0},{2,3},{3,2},{4,5},{5,4},{6,7},{7,6},{8,9},{9,8},{10,11... | collective-permute-start | bytes 1966088 | tf_op jit(solution)/shard_map/ppermute | solution.py:16
  76.4 4.8 %collective-permute-start.1 = (f32[2,2,16,64]{3,2,0,1:T(8,128)S(1)}, f32[2,2,16,64]{3,2,0,1:T(8,128)S(1)}, u32[]{:S(2)}, u32[]{:S(2)}) collective-permute-start(f32[2,2,16,64]{3,2,0,1:T(8,128)S(1)} %pad_maximum_fusion.13), channel_id=1, source_target_pairs={{0,8},{1,9},{2,10},{3,11},{4,12},{5,13},{6,14},{7,15},{8,0},{9,1},... | collective-permute-start | bytes 49160 | tf_op jit(solution)/shard_map/ppermute | solution.py:16
  86.9 5.0 %collective-permute-start.3 = (f32[8,2,16,64]{3,2,0,1:T(8,128)S(1)}, f32[8,2,16,64]{3,2,0,1:T(8,128)S(1)}, u32[]{:S(2)}, u32[]{:S(2)}) collective-permute-start(f32[8,2,16,64]{3,2,0,1:T(8,128)S(1)} %pad_maximum_fusion.11), channel_id=1, source_target_pairs={{0,1},{1,0},{2,3},{3,2},{4,5},{5,4},{6,7},{7,6},{8,9},{9,8},{10,11... | collective-permute-start | bytes 196616 | tf_op jit(solution)/shard_map/ppermute | solution.py:16
  92.0 51.1 %collective-permute-start.4 = (bf16[1,64,2048]{2,1,0:T(8,128)(2,1)S(1)}, bf16[1,64,2048]{2,1,0:T(8,128)(2,1)S(1)}, u32[]{:S(2)}, u32[]{:S(2)}) collective-permute-start(bf16[1,64,2048]{2,1,0:T(8,128)(2,1)S(1)} %copy-done.13), channel_id=1, source_target_pairs={{0,4},{1,5},{2,6},{3,7},{4,0},{5,1},{6,2},{7,3},{8,12},{9,13},{10,... | collective-permute-start | bytes 786440 | tf_op jit(solution)/shard_map/ppermute | solution.py:16
  139.9 49.8 %collective-permute-start.8 = (bf16[2,192,2048]{2,1,0:T(8,128)(2,1)}, bf16[2,192,2048]{2,1,0:T(8,128)(2,1)}, u32[]{:S(2)}, u32[]{:S(2)}) collective-permute-start(bf16[2,192,2048]{2,1,0:T(8,128)(2,1)} %dynamic-slice_bitcast_fusion.1), channel_id=1, source_target_pairs={{0,2},{1,3},{2,0},{3,1},{4,6},{5,7},{6,4},{7,5},{8,10},{9,11},{10,... | collective-permute-start | bytes 4718600 | tf_op jit(solution)/shard_map/ppermute | solution.py:16
  143.1 32.7 %collective-permute-start.18 = (bf16[2,64,2048]{2,1,0:T(8,128)(2,1)S(1)}, bf16[2,64,2048]{2,1,0:T(8,128)(2,1)S(1)}, u32[]{:S(2)}, u32[]{:S(2)}) collective-permute-start(bf16[2,64,2048]{2,1,0:T(8,128)(2,1)S(1)} %pad_maximum_fusion.10), channel_id=1, source_target_pairs={{0,8},{1,9},{2,10},{3,11},{4,12},{5,13},{6,14},{7,15},{8,0},{9,1},... | collective-permute-start | bytes 1572872 | tf_op jit(solution)/shard_map/ppermute | solution.py:16
  151.6 34.0 %collective-permute-start.5 = (bf16[2,64,2048]{2,1,0:T(8,128)(2,1)S(1)}, bf16[2,64,2048]{2,1,0:T(8,128)(2,1)S(1)}, u32[]{:S(2)}, u32[]{:S(2)}) collective-permute-start(bf16[2,64,2048]{2,1,0:T(8,128)(2,1)S(1)} %pad_maximum_fusion.9), channel_id=1, source_target_pairs={{0,8},{1,9},{2,10},{3,11},{4,12},{5,13},{6,14},{7,15},{8,0},{9,1},... | collective-permute-start | bytes 1572872 | tf_op jit(solution)/shard_map/ppermute | solution.py:16
  153.1 78.7 %collective-permute-start.29 = (bf16[2,160,2048]{2,1,0:T(8,128)(2,1)S(1)}, bf16[2,160,2048]{2,1,0:T(8,128)(2,1)S(1)}, u32[]{:S(2)}, u32[]{:S(2)}) collective-permute-start(bf16[2,160,2048]{2,1,0:T(8,128)(2,1)S(1)} %pad_maximum_fusion.5), channel_id=1, source_target_pairs={{0,1},{1,0},{2,3},{3,2},{4,5},{5,4},{6,7},{7,6},{8,9},{9,8},{10,11... | collective-permute-start | bytes 3932168 | tf_op jit(solution)/shard_map/ppermute | solution.py:16
  175.7 61.5 %collective-permute-start.27 = (bf16[2,160,2048]{2,1,0:T(8,128)(2,1)S(1)}, bf16[2,160,2048]{2,1,0:T(8,128)(2,1)S(1)}, u32[]{:S(2)}, u32[]{:S(2)}) collective-permute-start(bf16[2,160,2048]{2,1,0:T(8,128)(2,1)S(1)} %pad_maximum_fusion.4), channel_id=1, source_target_pairs={{0,2},{1,3},{2,0},{3,1},{4,6},{5,7},{6,4},{7,5},{8,10},{9,11},{10,... | collective-permute-start | bytes 3932168 | tf_op jit(solution)/shard_map/ppermute | solution.py:16
  185.6 23.8 %collective-permute-start.19 = (bf16[4,64,2048]{2,1,0:T(8,128)(2,1)S(1)}, bf16[4,64,2048]{2,1,0:T(8,128)(2,1)S(1)}, u32[]{:S(2)}, u32[]{:S(2)}) collective-permute-start(bf16[4,64,2048]{2,1,0:T(8,128)(2,1)S(1)} %pad_maximum_fusion.7), channel_id=1, source_target_pairs={{0,1},{1,0},{2,3},{3,2},{4,5},{5,4},{6,7},{7,6},{8,9},{9,8},{10,11... | collective-permute-start | bytes 3145736 | tf_op jit(solution)/shard_map/ppermute | solution.py:16
  187.2 42.7 %collective-permute-start.6 = (bf16[4,64,2048]{2,1,0:T(8,128)(2,1)S(1)}, bf16[4,64,2048]{2,1,0:T(8,128)(2,1)S(1)}, u32[]{:S(2)}, u32[]{:S(2)}) collective-permute-start(bf16[4,64,2048]{2,1,0:T(8,128)(2,1)S(1)} %pad_maximum_fusion.6), channel_id=1, source_target_pairs={{0,2},{1,3},{2,0},{3,1},{4,6},{5,7},{6,4},{7,5},{8,10},{9,11},{10,... | collective-permute-start | bytes 3145736 | tf_op jit(solution)/shard_map/ppermute | solution.py:16
  189.6 57.1 %collective-permute-start.11 = (bf16[192,2048]{1,0:T(8,128)(2,1)S(1)}, bf16[192,2048]{1,0:T(8,128)(2,1)S(1)}, u32[]{:S(2)}, u32[]{:S(2)}) collective-permute-start(bf16[192,2048]{1,0:T(8,128)(2,1)S(1)} %dynamic-slice_bitcast_fusion.2), channel_id=1, source_target_pairs={{0,2},{1,3},{2,0},{3,1},{4,6},{5,7},{6,4},{7,5},{8,10},{9,11},{10,... | collective-permute-start | bytes 2359304 | tf_op jit(solution)/shard_map/ppermute | solution.py:16
  209.5 76.5 %collective-permute-start.9 = (bf16[192,2048]{1,0:T(8,128)(2,1)}, bf16[192,2048]{1,0:T(8,128)(2,1)}, u32[]{:S(2)}, u32[]{:S(2)}) collective-permute-start(bf16[192,2048]{1,0:T(8,128)(2,1)} %dynamic-slice_bitcast_fusion.3), channel_id=1, source_target_pairs={{0,1},{1,0},{2,3},{3,2},{4,5},{5,4},{6,7},{7,6},{8,9},{9,8},{10,11... | collective-permute-start | bytes 2359304 | tf_op jit(solution)/shard_map/ppermute | solution.py:16
  229.9 73.7 %collective-permute-start.20 = (bf16[8,64,2048]{2,1,0:T(8,128)(2,1)S(1)}, bf16[8,64,2048]{2,1,0:T(8,128)(2,1)S(1)}, u32[]{:S(2)}, u32[]{:S(2)}) collective-permute-start(bf16[8,64,2048]{2,1,0:T(8,128)(2,1)S(1)} %pad_maximum_fusion.3), channel_id=1, source_target_pairs={{0,2},{1,3},{2,0},{3,1},{4,6},{5,7},{6,4},{7,5},{8,10},{9,11},{10,... | collective-permute-start | bytes 6291464 | tf_op jit(solution)/shard_map/ppermute | solution.py:16
  231.8 40.3 %collective-permute-start.7 = (bf16[8,64,2048]{2,1,0:T(8,128)(2,1)S(1)}, bf16[8,64,2048]{2,1,0:T(8,128)(2,1)S(1)}, u32[]{:S(2)}, u32[]{:S(2)}) collective-permute-start(bf16[8,64,2048]{2,1,0:T(8,128)(2,1)S(1)} %pad_maximum_fusion.2), channel_id=1, source_target_pairs={{0,1},{1,0},{2,3},{3,2},{4,5},{5,4},{6,7},{7,6},{8,9},{9,8},{10,11... | collective-permute-start | bytes 6291464 | tf_op jit(solution)/shard_map/ppermute | solution.py:16
  325.9 131.2 %all-to-all-start.1 = ((bf16[4,320,192]{1,2,0:T(8,128)(2,1)}), bf16[4,320,192]{1,2,0:T(8,128)(2,1)}, u32[]{:S(2)}, u32[]{:S(2)}) async-start(bf16[4,320,192]{1,2,0:T(8,128)(2,1)} %copy.88), calls=%async_computation.1 | async-start | bytes 1179648 | tf_op jit(solution)/shard_map/all_to_all | solution.py:210
  342.5 41.3 %collective-permute-start.21 = (bf16[8,64,2048]{2,1,0:T(8,128)(2,1)S(1)}, bf16[8,64,2048]{2,1,0:T(8,128)(2,1)S(1)}, u32[]{:S(2)}, u32[]{:S(2)}) collective-permute-start(bf16[8,64,2048]{2,1,0:T(8,128)(2,1)S(1)} %bitcast.259), channel_id=1, source_target_pairs={{0,2},{1,3},{2,0},{3,1},{4,6},{5,7},{6,4},{7,5},{8,10},{9,11},{10,... | collective-permute-start | bytes 6291464 | tf_op jit(solution)/shard_map/ppermute | solution.py:16
  346.3 46.5 %collective-permute-start.12 = (bf16[8,64,2048]{2,1,0:T(8,128)(2,1)S(1)}, bf16[8,64,2048]{2,1,0:T(8,128)(2,1)S(1)}, u32[]{:S(2)}, u32[]{:S(2)}) collective-permute-start(bf16[8,64,2048]{2,1,0:T(8,128)(2,1)S(1)} %bitcast.258), channel_id=1, source_target_pairs={{0,1},{1,0},{2,3},{3,2},{4,5},{5,4},{6,7},{7,6},{8,9},{9,8},{10,11... | collective-permute-start | bytes 6291464 | tf_op jit(solution)/shard_map/ppermute | solution.py:16
  384.7 23.6 %collective-permute-start.22 = (bf16[4,64,2048]{2,1,0:T(8,128)(2,1)S(1)}, bf16[4,64,2048]{2,1,0:T(8,128)(2,1)S(1)}, u32[]{:S(2)}, u32[]{:S(2)}) collective-permute-start(bf16[4,64,2048]{2,1,0:T(8,128)(2,1)S(1)} %slice.359), channel_id=1, source_target_pairs={{0,1},{1,0},{2,3},{3,2},{4,5},{5,4},{6,7},{7,6},{8,9},{9,8},{10,11... | collective-permute-start | bytes 3145736 | tf_op jit(solution)/shard_map/ppermute | solution.py:16
  393.7 15.9 %collective-permute-start.13 = (bf16[4,64,2048]{2,1,0:T(8,128)(2,1)S(1)}, bf16[4,64,2048]{2,1,0:T(8,128)(2,1)S(1)}, u32[]{:S(2)}, u32[]{:S(2)}) collective-permute-start(bf16[4,64,2048]{2,1,0:T(8,128)(2,1)S(1)} %slice.332), channel_id=1, source_target_pairs={{0,2},{1,3},{2,0},{3,1},{4,6},{5,7},{6,4},{7,5},{8,10},{9,11},{10,... | collective-permute-start | bytes 3145736 | tf_op jit(solution)/shard_map/ppermute | solution.py:16
  409.6 29.1 %collective-permute-start.23 = (bf16[2,64,2048]{2,1,0:T(8,128)(2,1)}, bf16[2,64,2048]{2,1,0:T(8,128)(2,1)S(1)}, u32[]{:S(2)}, u32[]{:S(2)}) collective-permute-start(bf16[2,64,2048]{2,1,0:T(8,128)(2,1)} %slice.361), channel_id=1, source_target_pairs={{0,8},{1,9},{2,10},{3,11},{4,12},{5,13},{6,14},{7,15},{8,0},{9,1},... | collective-permute-start | bytes 1572872 | tf_op jit(solution)/shard_map/ppermute | solution.py:16
  410.9 39.2 %collective-permute-start.14 = (bf16[2,64,2048]{2,1,0:T(8,128)(2,1)}, bf16[2,64,2048]{2,1,0:T(8,128)(2,1)}, u32[]{:S(2)}, u32[]{:S(2)}) collective-permute-start(bf16[2,64,2048]{2,1,0:T(8,128)(2,1)} %slice.334), channel_id=1, source_target_pairs={{0,8},{1,9},{2,10},{3,11},{4,12},{5,13},{6,14},{7,15},{8,0},{9,1},... | collective-permute-start | bytes 1572872 | tf_op jit(solution)/shard_map/ppermute | solution.py:16
  440.7 25.6 %collective-permute-start.24 = (bf16[1,64,2048]{2,1,0:T(8,128)(2,1)S(1)}, bf16[1,64,2048]{2,1,0:T(8,128)(2,1)}, u32[]{:S(2)}, u32[]{:S(2)}) collective-permute-start(bf16[1,64,2048]{2,1,0:T(8,128)(2,1)S(1)} %slice.363), channel_id=1, source_target_pairs={{0,4},{1,5},{2,6},{3,7},{4,0},{5,1},{6,2},{7,3},{8,12},{9,13},{10,... | collective-permute-start | bytes 786440 | tf_op jit(solution)/shard_map/ppermute | solution.py:16
  452.9 13.4 %collective-permute-start.15 = (bf16[1,64,2048]{2,1,0:T(8,128)(2,1)}, bf16[1,64,2048]{2,1,0:T(8,128)(2,1)}, u32[]{:S(2)}, u32[]{:S(2)}) collective-permute-start(bf16[1,64,2048]{2,1,0:T(8,128)(2,1)} %slice.336), channel_id=1, source_target_pairs={{0,4},{1,5},{2,6},{3,7},{4,0},{5,1},{6,2},{7,3},{8,12},{9,13},{10,... | collective-permute-start | bytes 786440 | tf_op jit(solution)/shard_map/ppermute | solution.py:16
  457.1 15.6 %all-to-all-start.2 = ((bf16[192,4,512]{2,0,1:T(8,128)(2,1)}), bf16[192,4,512]{2,0,1:T(8,128)(2,1)}, u32[]{:S(2)}, u32[]{:S(2)}) async-start(bf16[192,4,512]{2,0,1:T(8,128)(2,1)} %bitcast.251), calls=%async_computation.2 | async-start | bytes 1572864 | tf_op jit(solution)/shard_map/all_to_all | solution.py:206
  468.4 6.6 %collective-permute-start.16 = (bf16[64,2048]{1,0:T(8,128)(2,1)}, bf16[64,2048]{1,0:T(8,128)(2,1)S(1)}, u32[]{:S(2)}, u32[]{:S(2)}) collective-permute-start(bf16[64,2048]{1,0:T(8,128)(2,1)} %get-tuple-element.52), channel_id=1, source_target_pairs={{16,0},{0,16},{17,1},{1,17},{18,2},{2,18},{19,3},{3,19},{20,4},{4,... | collective-permute-start | bytes 786440 | tf_op jit(solution)/shard_map/ppermute | solution.py:22
  468.4 6.6 %collective-permute-start.25 = (bf16[64,2048]{1,0:T(8,128)(2,1)S(1)}, bf16[64,2048]{1,0:T(8,128)(2,1)S(1)}, u32[]{:S(2)}, u32[]{:S(2)}) collective-permute-start(bf16[64,2048]{1,0:T(8,128)(2,1)S(1)} %get-tuple-element.53), channel_id=1, source_target_pairs={{16,0},{0,16},{17,1},{1,17},{18,2},{2,18},{19,3},{3,19},{20,4},{4,... | collective-permute-start | bytes 786440 | tf_op jit(solution)/shard_map/ppermute | solution.py:22
  (52 other events, 452.4 us)
